TPU v7x, 256 devices: a whole 4x4x8 slice. The times are simulated.
256 devices in a mesh: img: 16 (over z, core), pos: 16 (over x, y).
Axes of the slice: x: 4, y: 4, z: 8, core: 2. Of those that a mesh axis runs over, the one named last changes fastest.
Arguments:
- section_one: bfloat16 [512, 28, 28, 64], P(('img', 'pos')), may hold values from -6 to 6
- section_two: bfloat16 [512, 14, 14, 128], P(('img', 'pos')), may hold values from -6 to 6
- section_three: bfloat16 [512, 7, 7, 256], P(('img', 'pos')), may hold values from -6 to 6
- weight_one: bfloat16 [3, 3, 64, 64], replicated, may hold values from -0.25 to 0.25
- weight_two: bfloat16 [3, 3, 128, 128], replicated, may hold values from -0.1875 to 0.1875
- weight_three: bfloat16 [3, 3, 256, 256], replicated, may hold values from -0.125 to 0.125
- gain_one: float32 [64], replicated, may hold values from 0.25 to 1.75
- gain_two: float32 [128], replicated, may hold values from 0.25 to 1.75
- gain_three: float32 [256], replicated, may hold values from 0.25 to 1.75
- bias_one: float32 [64], replicated, may hold values from -3 to 3
- bias_two: float32 [128], replicated, may hold values from -3 to 3
- bias_three: float32 [256], replicated, may hold values from -3 to 3
- channel_index: int32 [100], replicated, may hold values from 0 to 447, as said below
- valid_count: int32 [16, 16], P('img', 'pos'), may hold values from 1 to 2, as said below
Outputs:
- mean: float32 [100, 784], P(None, 'pos')
- covariance: float32 [784, 10000], P('pos')
Inputs may be any that keep to these rules, and one draw needn't show every extreme that they name: `channel_index`: 100 distinct channel numbers; 0 and 447 are always among them. `valid_count`: A device's valid images are its first slots. Every draw has a device with 2 valid images and one with 1.
All inputs are finite; a program needn't handle non-finite values.
Results may differ from a plain program's by a relative error of at most 0.0022.
Values may be sent and summed in bfloat16 or wider, within the bound.
A program may use at most 128 MiB of HBM per device.

v0:
```python
from functools import partial

import jax
import jax.numpy as jnp
from jax import lax
from jax.sharding import PartitionSpec as P


def merged(part, axis, combine):
    gathered = jax.tree.map(lambda a: lax.all_gather(a, axis), part)

    def take(source):
        return jax.tree.map(lambda a: lax.dynamic_index_in_dim(a, source, 0, False), gathered)

    return lax.fori_loop(
        1, lax.axis_size(axis), lambda source, state: combine(state, take(source)), take(0)
    )


def section_out(images, weight, gain, bias):
    conv = lax.conv_general_dilated(
        images,
        weight,
        (1, 1),
        "SAME",
        dimension_numbers=("NHWC", "HWIO", "NHWC"),
        preferred_element_type=jnp.float32,
    )
    return jax.nn.relu(conv * gain + bias).astype(jnp.bfloat16)


def pick_channels(section, offset, width, channel_index):
    table = (channel_index[None, :] - offset == lax.iota(jnp.int32, width)[:, None]).astype(
        jnp.bfloat16
    )
    return jnp.einsum("ihwc,ck->ikhw", section, table, preferred_element_type=jnp.float32).astype(
        jnp.bfloat16
    )


def widen(picked, factor):
    return jnp.repeat(jnp.repeat(picked, factor, axis=2), factor, axis=3)


def pair_outer(rows):
    return (rows[:, :, None] * rows[:, None, :]).reshape(
        rows.shape[0], rows.shape[1] * rows.shape[1]
    )


def product_rows(values):
    kept = values.shape[1]
    raw = jnp.einsum("ikp,ilp->pkl", values, values, preferred_element_type=jnp.float32)
    return raw.reshape(values.shape[2], kept * kept)


def moments(piece):
    values = piece[:, :, 0, :]
    sums = jnp.sum(values, axis=0, dtype=jnp.float32).T[None]
    return (sums, product_rows(values)[None])


def chan_pair(outer_fn, left, right):
    count_left, mean_left, moment_left = left
    count_right, mean_right, moment_right = right
    joined = count_left + count_right
    delta = mean_right - mean_left
    merged_mean = mean_left + delta * (count_right / joined)
    merged_moment = (
        moment_left + moment_right + outer_fn(delta) * (count_left * count_right / joined)
    )
    return (joined, merged_mean, merged_moment)


def per_device(
    section_one,
    section_two,
    section_three,
    weight_one,
    weight_two,
    weight_three,
    gain_one,
    gain_two,
    gain_three,
    bias_one,
    bias_two,
    bias_three,
    channel_index,
    valid_count,
):
    slots = section_one.shape[0]
    side = section_one.shape[1]
    width_one = section_one.shape[3]
    width_two = section_two.shape[3]
    width_three = section_three.shape[3]
    kept = channel_index.shape[0]
    owners = lax.axis_size("pos")
    block = side * side // owners
    own_count = valid_count[0, 0]
    scale = (lax.iota(jnp.int32, slots) < own_count).astype(jnp.bfloat16)[:, None, None, None]
    out_one = section_out(section_one, weight_one, gain_one, bias_one) * scale
    out_two = section_out(section_two, weight_two, gain_two, bias_two) * scale
    out_three = section_out(section_three, weight_three, gain_three, bias_three) * scale
    features = pick_channels(out_one, 0, width_one, channel_index)
    features = features + widen(pick_channels(out_two, width_one, width_two, channel_index), 2)
    features = features + widen(
        pick_channels(out_three, width_one + width_two, width_three, channel_index), 4
    )
    shaped = features.reshape(slots, kept, owners, block)
    group = lax.psum(own_count, "pos").astype(jnp.float32)
    sums, raw = moments(lax.all_to_all(shaped, "pos", split_axis=2, concat_axis=0, tiled=True))
    local_mean = sums[0] / group
    centered = raw[0] - group * pair_outer(local_mean)
    total, mean, packed = merged(
        (group, local_mean, centered), "img", partial(chan_pair, pair_outer)
    )
    covariance = packed / (total - 1.0) + 0.01 * jnp.eye(kept, dtype=jnp.float32).reshape(
        1, kept * kept
    )
    return (mean.T, covariance)


def solution(mesh):
    return jax.shard_map(
        per_device,
        mesh=mesh,
        in_specs=(
            P(("img", "pos"), None, None, None),
            P(("img", "pos"), None, None, None),
            P(("img", "pos"), None, None, None),
            P(),
            P(),
            P(),
            P(),
            P(),
            P(),
            P(),
            P(),
            P(),
            P(),
            P("img", "pos"),
        ),
        out_specs=(P(None, "pos"), P("pos", None)),
        check_vma=False,
    )
```

profile of v0, /device:TPU:1, one launch (start us, length us, event | category | flops | bytes accessed | tf_op | source)
XLA Modules:
  0.0 435.1 jit_solution(2955952425965308165)
XLA Ops:
  15.9 7.6 %all-to-all-start = ((bf16[2,100,16,49]{1,0,3,2:T(2,128)(2,1)}), bf16[2,100,16,49]{1,0,3,2:T(2,128)(2,1)S(1)}, u32[]{:S(2)}, u32[]{:S(2)}) async-start(bf16[2,100,16,49]{1,0,3,2:T(2,128)(2,1)} %bitcast.32), calls=%async_computation | async-start | bytes 802816 | tf_op jit(solution)/shard_map/all_to_all | solution.py:111
  23.6 14.7 %psum.7 = s32[]{:T(128)} all-reduce(s32[]{:T(128)} %bitcast.3), channel_id=1, replica_groups=mesh['img'=16,'pos'=16] {'pos'}, use_global_device_ids=true, to_apply=%region_0.1 | all-reduce | flops 1 | bytes 8 | tf_op jit(solution)/shard_map/psum | solution.py:110
  39.7 2.4 multiply_subtract_fusion
  42.1 3.5 sub.37
  47.5 31.3 %all-reduce = f32[16]{0:T(128)S(1)} all-reduce(f32[16]{0:T(128)S(1)} %dynamic-update-slice), channel_id=1, replica_groups=mesh['img'=16,'pos'=16] {'img'}, use_global_device_ids=true, to_apply=%add | all-reduce | flops 16 | bytes 128
  79.0 19.6 %all-gather.1 = f32[16,49,100]{2,1,0:T(8,128)} all-gather(f32[1,49,100]{2,1,0:T(8,128)S(1)} %get-tuple-element.200), channel_id=2, replica_groups=mesh['img'=16,'pos'=16] {'img'}, dimensions={0}, use_global_device_ids=true | all-gather | bytes 333200 | tf_op jit(solution)/shard_map/all_gather | solution.py:10
  99.4 138.8 %all-gather.4.cloned.1.call-done = f32[16,49,10000]{2,1,0:T(8,128)} async-done(((f32[1,49,10000]{2,1,0:T(8,128)}), f32[16,49,10000]{2,1,0:T(8,128)}) %all-gather.4.cloned.1.call-update) | async-done | bytes 31360016 | tf_op jit(solution)/shard_map/all_gather | solution.py:10
  238.2 3.2 slice_bitcast_fusion
  241.3 183.8 %while.19 = (s32[]{:T(128)}, f32[]{:T(128)}, f32[49,100]{1,0:T(8,128)S(1)}, f32[49,10000]{1,0:T(8,128)}, f32[16]{0:T(128)S(1)}, /*index=5*/f32[16,49,100]{2,1,0:...) while((s32[]{:T(128)}, f32[]{:T(128)}, f32[49,100]{1,0:T(8,128)S(1)}, ...), condition=%wide.region_3.4_spmd, body=%wide.region_2.3_spmd.sunk | while | flops 1974709 | bytes 13818227 | solution.py:15
  244.9 2.0 multiply_multiply_fusion.2
  246.9 2.7 mul.244
  249.6 4.0 fusion.63
  257.1 2.0 multiply_multiply_fusion.2
  259.1 2.7 mul.244
  261.8 4.0 fusion.63
  269.4 2.0 multiply_multiply_fusion.2
  271.4 2.7 mul.244
  274.1 4.0 fusion.63
  281.6 2.0 multiply_multiply_fusion.2
  283.6 2.7 mul.244
  286.3 4.0 fusion.63
  293.9 2.0 multiply_multiply_fusion.2
  295.9 2.7 mul.244
  298.6 4.0 fusion.63
  306.1 2.0 multiply_multiply_fusion.2
  308.1 2.7 mul.244
  310.8 4.0 fusion.63
  318.4 2.0 multiply_multiply_fusion.2
  320.4 2.7 mul.244
  323.1 4.0 fusion.63
  330.6 2.0 multiply_multiply_fusion.2
  332.6 2.7 mul.244
  335.3 4.0 fusion.63
  344.9 2.7 mul.244
  347.6 4.0 fusion.63
  357.1 2.7 mul.244
  359.8 4.0 fusion.63
  369.4 2.7 mul.244
  372.1 4.0 fusion.63
  381.6 2.7 mul.244
  384.3 4.0 fusion.63
  393.9 2.7 mul.244
  396.6 4.0 fusion.63
  406.1 2.7 mul.244
  408.8 4.0 fusion.63
  418.4 2.7 mul.244
  421.1 4.0 fusion.63
  425.1 3.2 divide_add_fusion
  (102 shorter events, 46.5 us)
Async XLA Ops:
  7.2 1.5 copy-start
  7.2 3.4 copy-start.13
  7.2 3.1 copy-start.3
  7.2 3.4 copy-start.5
  7.2 3.4 copy-start.7
  7.2 3.4 copy-start.8
  8.7 2.9 copy-start.2
  10.6 1.8 copy-start.6
  10.6 1.8 copy-start.9
  10.6 1.8 copy-start.10
  10.7 1.8 copy-start.12
  12.5 1.1 copy-start.4
  15.9 23.0 %all-to-all-start = ((bf16[2,100,16,49]{1,0,3,2:T(2,128)(2,1)}), bf16[2,100,16,49]{1,0,3,2:T(2,128)(2,1)S(1)}, u32[]{:S(2)}, u32[]{:S(2)}) async-start(bf16[2,100,16,49]{1,0,3,2:T(2,128)(2,1)} %bitcast.32), calls=%async_computation | async-start | bytes 802816 | tf_op jit(solution)/shard_map/all_to_all | solution.py:111
  23.5 214.7 %all-gather.4.cloned.1.call-start = ((), (), s32[]{:S(2)}) async-start(), calls=%async_computation.1 | async-start | bytes 38506496 | tf_op jit(solution)/shard_map/all_gather | solution.py:10
  45.6 0.7 copy-start.11
  425.1 3.2 copy-start.1
Sparse Core Ops, SparseCore 0:
  45.7 192.3 all-gather.3
where the time goes:
time: 438 us; the launch traced here: 435 us
  waiting for transfers between devices  139 us (32%)
  other arithmetic  107 us (24%)
  blocking collectives  65.6 us (15%)
  local copies, waits for them, and re-layouts  62.1 us (14%)
  loops' own time  32 us (7%)
  between operations  15.9 us (4%)
  starting transfers between devices  7.62 us (2%)
  matrix products  5.81 us (1%)
    all_gather x1, waiting for transfers between devices, merged(): gathered = jax.tree.map(lambda a: lax.all_gather(a, axis), part)  139 us
    add x15, other arithmetic, chan_pair(): moment_left + moment_right  60.3 us
    mul x15, local copies, waits for them, and re-layouts, chan_pair(): outer_fn(delta) * (count_left * count_right / joined)  40.4 us
    another operation x1, loops' own time, merged(): lax.fori_loop(1, lax.axis_size(axis), lambda source, state: combine(state...  32 us
    unnamed x1, blocking collectives  31.3 us
    mul x15, other arithmetic, chan_pair(): outer_fn(delta) * (count_left * count_right / joined)  29.8 us
    all_gather x1, blocking collectives, merged(): gathered = jax.tree.map(lambda a: lax.all_gather(a, axis), part)  19.6 us
    psum x1, blocking collectives, per_device(): group = lax.psum(own_count, 'pos').astype(jnp.float32)  14.7 us
  transfers between devices with their start and end apart: 2, of which 1 were waited for; matrix products, arithmetic and copies ran while one was open for 0% of the time, Pallas kernels for 0%

commit v1 on v0

v1 whole, which is shorter than its diff:
```python
import functools

import jax
import jax.numpy as jnp
import numpy as np
from jax import lax
from jax.experimental import pallas as pl
from jax.experimental.pallas import tpu as pltpu
from jax.sharding import PartitionSpec as P

MESH = pl.DeviceIdType.MESH
LANES = 128
ONES = 127
SLOTS = 4
UNIT = 8
FLAT = 80
WINDOW = 320


def section_out(images, weight, gain, bias):
    conv = lax.conv_general_dilated(
        images,
        weight,
        (1, 1),
        "SAME",
        dimension_numbers=("NHWC", "HWIO", "NHWC"),
        preferred_element_type=jnp.float32,
    )
    return jax.nn.relu(conv * gain + bias).astype(jnp.bfloat16)


def pick_channels(section, offset, slots):
    width = section.shape[3]
    table = (slots[None, :] - offset == lax.iota(jnp.int32, width)[:, None]).astype(jnp.bfloat16)
    return jnp.einsum(
        "ihwc,ck->ihwk", section, table, preferred_element_type=jnp.float32
    ).astype(jnp.bfloat16)


def gather_table(side, blocks, sharers):
    block = side * side // blocks
    own = block // sharers
    table = np.zeros((blocks, sharers * UNIT, WINDOW), np.float32)
    for j in range(blocks):
        y0 = j * block // side
        for i in range(sharers):
            for q in range(SLOTS):
                position = j * block + (i * own + q if q < own else block - 1)
                y, x = divmod(position, side)
                for g in range(2):
                    row = i * UNIT + q * 2 + g
                    table[j, row, g * 96 + (y - y0) * 32 + x] = 1
                    table[j, row, 192 + g * 32 + (y // 2 - y0 // 2) * 16 + x // 2] = 1
                    table[j, row, 256 + g * 32 + (y // 4 - y0 // 4) * 16 + x // 4] = 1
    return table.astype(jnp.bfloat16)


def iota(shape, dim):
    return lax.broadcasted_iota(jnp.int32, shape, dim)


def flatten_tables(kept):
    f = iota((FLAT, LANES), 0) * LANES
    k = iota((FLAT, LANES), 1)
    picks, masks = [], []
    start = jnp.floor((f.astype(jnp.float32) + 0.5) * (1.0 / kept))
    rest = f - start.astype(jnp.int32) * kept + k
    for t in range(3):
        picks.append(((k - t) * kept <= f) & (f < (k - t + 1) * kept))
        masks.append((rest >= t * kept) & (rest < (t + 1) * kept))
    return jnp.concatenate(picks, 0), masks


def kernel(
    kept,
    f1_ref,
    f2_ref,
    f3_ref,
    table_ref,
    out_ref,
    last_ref,
    s_ref,
    r1_ref,
    r2_ref,
    a_send,
    a_recv,
    b_send,
    b_recv,
    cw_send,
    cw_recv,
    ccw_send,
    ccw_recv,
    pair_send,
    pair_recv,
):
    groups, owners = s_ref.shape[:2]
    chips = groups // 2
    me = lax.axis_index("img")
    my_pos = lax.axis_index("pos")
    z, core = me // 2, me % 2

    barrier = pltpu.get_barrier_semaphore()

    @pl.loop(1, groups)
    def _(d):
        pl.semaphore_signal(
            barrier, inc=1, device_id=(lax.rem(me + d, groups), my_pos), device_id_type=MESH
        )

    @pl.loop(1, owners)
    def _(d):
        pl.semaphore_signal(
            barrier, inc=1, device_id=(me, lax.rem(my_pos + d, owners)), device_id_type=MESH
        )

    @pl.loop(0, owners)
    def _(j):
        y0 = (7 * j) // 4
        parts = []
        for ref, y, rows in ((f1_ref, y0, 3), (f2_ref, y0 // 2, 2), (f3_ref, y0 // 4, 2)):
            for g in range(2):
                parts.append(ref[g, pl.ds(y, rows)].reshape(-1, LANES))
        picked = jnp.dot(
            table_ref[j], jnp.concatenate(parts, 0), preferred_element_type=jnp.float32
        )
        s_ref[:, j] = picked.reshape(groups, UNIT, LANES).astype(jnp.bfloat16)

    pl.semaphore_wait(barrier, groups - 1 + owners - 1)

    def to_group(d):
        target = lax.rem(me + d, groups)
        return pltpu.make_async_remote_copy(
            src_ref=s_ref.at[target],
            dst_ref=r1_ref.at[me],
            send_sem=a_send.at[d],
            recv_sem=a_recv.at[d],
            device_id=(target, my_pos),
            device_id_type=MESH,
        )

    def to_owner(d):
        target = lax.rem(my_pos + d, owners)
        return pltpu.make_async_remote_copy(
            src_ref=r1_ref.at[:, target],
            dst_ref=r2_ref.at[my_pos],
            send_sem=b_send.at[d],
            recv_sem=b_recv.at[d],
            device_id=(me, target),
            device_id_type=MESH,
        )

    @pl.loop(1, groups)
    def _(d):
        to_group(d).start()

    r1_ref[me] = s_ref[me]

    @pl.loop(1, groups)
    def _(d):
        to_group(d).wait()

    @pl.loop(1, owners)
    def _(d):
        to_owner(d).start()

    r2_ref[my_pos] = r1_ref[:, my_pos]

    picks, masks = flatten_tables(kept)
    picks = jnp.where(picks, 1.0, 0.0).astype(jnp.bfloat16)

    @pl.loop(1, owners)
    def _(d):
        to_owner(d).wait()

    rows = groups * owners * UNIT
    x = r2_ref[...].astype(jnp.float32).reshape(rows, LANES)
    slot = (iota((rows, LANES), 0) >> 1) & (SLOTS - 1)
    spread = jnp.concatenate([jnp.where(slot == q, x, 0.0) for q in range(SLOTS)], 1)
    gram = lax.dot_general(
        x.astype(jnp.bfloat16),
        spread.astype(jnp.bfloat16),
        (((0,), (0,)), ((), ())),
        preferred_element_type=jnp.float32,
    )

    k = iota((LANES, LANES), 0)
    eye = jnp.where(k == iota((LANES, LANES), 1), 0.01, 0.0)
    turn = k * kept
    rolled, means = [], []
    for q in range(SLOTS):
        raw = gram[:, q * LANES : (q + 1) * LANES]
        total = raw[ONES:, ONES:]
        mean = raw[ONES:, :] / total
        cov = (raw - raw[:, ONES:] * mean) / (total - 1.0) + eye
        for bit in (4, 8, 16, 32, 64):
            cov = jnp.where((turn & bit) != 0, pltpu.roll(cov, bit, 1), cov)
        rolled.append(cov.astype(jnp.bfloat16))
        means.append(mean)
    flat = jnp.dot(picks, jnp.concatenate(rolled, 1), preferred_element_type=jnp.float32)

    row, lane = iota((FLAT, LANES), 0), iota((FLAT, LANES), 1)
    used = kept * kept
    edge = used % LANES
    for q in range(SLOTS):
        packet = jnp.zeros((FLAT, LANES), jnp.float32)
        for t in range(3):
            part = flat[t * FLAT : (t + 1) * FLAT, q * LANES : (q + 1) * LANES]
            packet = packet + jnp.where(masks[t], part, 0.0)
        high = means[q].astype(jnp.bfloat16).astype(jnp.float32)
        low = pltpu.roll(jnp.broadcast_to(means[q] - high, (8, LANES)), edge, 1)[:1]
        packet = jnp.where(row == FLAT - 1, high, packet)
        packet = jnp.where((row == FLAT - 2) & (lane >= edge), low, packet)
        packet = packet.astype(jnp.bfloat16)
        if q < SLOTS - 1:
            out_ref[me, q * FLAT : (q + 1) * FLAT] = packet
        else:
            last_ref[...] = packet

    def send(chip, sems, step, device):
        part = out_ref.at[chip * 2 + core]
        copy = pltpu.make_async_remote_copy(
            src_ref=part,
            dst_ref=part,
            send_sem=sems[0].at[step],
            recv_sem=sems[1].at[step],
            device_id=device,
            device_id_type=MESH,
        )
        copy.start()
        return copy

    right = (lax.rem(z + 1, chips) * 2 + core, my_pos)
    left = (lax.rem(z + chips - 1, chips) * 2 + core, my_pos)
    partner = (z * 2 + 1 - core, my_pos)
    cw_sems, ccw_sems, pair_sems = (cw_send, cw_recv), (ccw_send, ccw_recv), (pair_send, pair_recv)
    half = chips // 2
    cw = send(z, cw_sems, 0, right)
    ccw = send(z, ccw_sems, 0, left)
    pairs = [send(z, pair_sems, 0, partner)]
    sent = [cw, ccw]
    for step in range(1, half + 1):
        came = lax.rem(z + chips - step, chips)
        cw.wait_recv()
        if step < half:
            cw = send(came, cw_sems, step, right)
            sent.append(cw)
        pairs.append(send(came, pair_sems, step, partner))
        if step < half:
            came = lax.rem(z + step, chips)
            ccw.wait_recv()
            if step < half - 1:
                ccw = send(came, ccw_sems, step, left)
                sent.append(ccw)
            pairs.append(send(came, pair_sems, half + step, partner))
    for copy in sent:
        copy.wait_send()
    for copy in pairs:
        copy.wait()


def per_device(
    section_one,
    section_two,
    section_three,
    weight_one,
    weight_two,
    weight_three,
    gain_one,
    gain_two,
    gain_three,
    bias_one,
    bias_two,
    bias_three,
    channel_index,
    valid_count,
):
    images, side = section_one.shape[:2]
    width_one, width_two = section_one.shape[3], section_two.shape[3]
    kept = channel_index.shape[0]
    groups, owners = lax.axis_size("img"), lax.axis_size("pos")
    block = side * side // owners
    scale = (lax.iota(jnp.int32, images) < valid_count[0, 0]).astype(jnp.bfloat16)
    scale = scale[:, None, None, None]
    out_one = section_out(section_one, weight_one, gain_one, bias_one) * scale
    out_two = section_out(section_two, weight_two, gain_two, bias_two) * scale
    out_three = section_out(section_three, weight_three, gain_three, bias_three) * scale
    slots = jnp.pad(channel_index, (0, LANES - kept), constant_values=-1024)
    f1 = pick_channels(out_one, 0, slots)
    f1 = jnp.where(lax.iota(jnp.int32, LANES) == ONES, scale, f1)
    f2 = pick_channels(out_two, width_one, slots)
    f3 = pick_channels(out_three, width_one + width_two, slots)
    f1 = jnp.pad(f1, ((0, 0), (0, 1), (0, 4), (0, 0)))
    f2 = jnp.pad(f2, ((0, 0), (0, 2), (0, 2), (0, 0)))
    f3 = jnp.pad(f3, ((0, 0), (0, 1), (0, 9), (0, 0)))
    table = jnp.asarray(gather_table(side, owners, groups))
    own = SLOTS - 1
    vmem = pl.BlockSpec(memory_space=pltpu.VMEM)
    dma = pltpu.SemaphoreType.DMA
    out, last = pl.pallas_call(
        functools.partial(kernel, kept),
        out_shape=(
            jax.ShapeDtypeStruct((groups, own * FLAT, LANES), jnp.bfloat16),
            jax.ShapeDtypeStruct((FLAT, LANES), jnp.bfloat16),
        ),
        in_specs=[vmem] * 4,
        out_specs=[vmem] * 2,
        scratch_shapes=[
            pltpu.VMEM((groups, owners, UNIT, LANES), jnp.bfloat16),
            pltpu.VMEM((groups, owners, UNIT, LANES), jnp.bfloat16),
            pltpu.VMEM((owners, groups, UNIT, LANES), jnp.bfloat16),
            dma((groups,)),
            dma((groups,)),
            dma((owners,)),
            dma((owners,)),
            dma((groups // 4,)),
            dma((groups // 4,)),
            dma((groups // 4,)),
            dma((groups // 4,)),
            dma((groups // 2,)),
            dma((groups // 2,)),
        ],
        compiler_params=pltpu.CompilerParams(
            collective_id=0, has_side_effects=True, vmem_limit_bytes=40 * 2**20
        ),
        cost_estimate=pl.CostEstimate(
            flops=800_000_000, bytes_accessed=4_000_000, transcendentals=0
        ),
        name="statistics",
    )(f1, f2, f3, table)
    packets = jnp.concatenate(
        [out.reshape(block - 1, FLAT * LANES), last.reshape(1, FLAT * LANES)]
    ).astype(jnp.float32)
    used = kept * kept
    covariance = packets[:, :used]
    end = (FLAT - 1) * LANES
    mean = packets[:, end : end + kept] + packets[:, used : used + kept]
    return (mean.T, covariance)


def solution(mesh):
    return jax.shard_map(
        per_device,
        mesh=mesh,
        in_specs=(P(("img", "pos"), None, None, None),) * 3
        + (P(),) * 10
        + (P("img", "pos"),),
        out_specs=(P(None, "pos"), P("pos", None)),
        check_vma=False,
    )
```

time: 438 us -> 60.4 us (0.14)
  waiting for transfers between devices: 139 us -> 0 us
  other arithmetic: 107 us -> 2.89 us
  blocking collectives: 65.6 us -> 0 us
  local copies, waits for them, and re-layouts: 62.1 us -> 1.67 us
  Pallas kernels: 0 us -> 49.6 us
  loops' own time: 32 us -> 0 us
  between operations: 15.9 us -> 1.64 us
  starting transfers between devices: 7.62 us -> 0 us
    all_gather x1 -> x0, waiting for transfers between devices: 139 us -> none  [merged(): gathered = jax.tree.map(lambda a: lax.all_gather(a, axis), part)]
    add x32 -> x0, other arithmetic: 76.4 us -> none  [the longest x15 60.3 us: chan_pair(): moment_left + moment_right]
    pallas_call x0 -> x1, Pallas kernels: none -> 49.6 us  [per_device(): pl.pallas_call(functools.partial(kernel, kept), out_shape=(jax.ShapeDtype...]
    mul x20 -> x0, local copies, waits for them, and re-layouts: 41 us -> none  [the longest x15 40.4 us: chan_pair(): outer_fn(delta) * (count_left * count_right / joined)]
    another operation x1 -> x0, loops' own time: 32 us -> none  [merged(): lax.fori_loop(1, lax.axis_size(axis), lambda source, state: combine(state...]
    unnamed x1 -> x0, blocking collectives: 31.3 us -> none
    mul x16 -> x0, other arithmetic: 29.8 us -> none  [the longest x15 29.8 us: chan_pair(): outer_fn(delta) * (count_left * count_right / joined)]
    all_gather x1 -> x0, blocking collectives: 19.6 us -> none  [merged(): gathered = jax.tree.map(lambda a: lax.all_gather(a, axis), part)]
  transfers between devices with their start and end apart: 2 -> 0, of which waited for: 1 -> 0; matrix products, arithmetic and copies ran while one was open for 0% -> 0% of each run, Pallas kernels for 0% -> 0%
where the time goes in v1:
time: 60.4 us; the launch traced here: 60.2 us
  Pallas kernels  49.6 us (82%)
  matrix products  4.42 us (7%)
  other arithmetic  2.89 us (5%)
  local copies, waits for them, and re-layouts  1.67 us (3%)
  between operations  1.64 us (3%)
    pallas_call x1, Pallas kernels, per_device(): pl.pallas_call(functools.partial(kernel, kept), out_shape=(jax.ShapeDtype...  49.6 us
    conv_general_dilated x3, matrix products, section_out(): lax.conv_general_dilated(images, weight, (1, 1), 'SAME', dimension_number...  3.82 us
    convert_element_type x1, other arithmetic, per_device(): packets = jnp.concatenate([out.reshape(block - 1, FLAT * LANES), last.res...  1.53 us

profile of v1, /device:TPU:1, one launch (start us, length us, event | category | flops | bytes accessed | tf_op | source)
XLA Modules:
  0.0 60.2 jit_solution(3302283515207281948)
XLA Ops:
  0.6 0.0 copy-start
  0.6 0.0 copy-start.6
  0.7 0.0 copy-start.7
  0.7 0.0 copy-start.3
  0.7 0.0 copy-start.5
  1.5 0.7 %broadcast_add_fusion = (s32[128]{0:T(128)S(1)}, s32[128]{0:T(128)S(1)}, s32[128]{0:T(128)S(1)}) fusion(s32[100]{0:T(128)} %param.27), kind=kLoop, calls=%fused_computation.38 | loop fusion | flops 256 | bytes 1936 | tf_op jit(solution)/shard_map/sub | solution.py:34
  2.1 0.0 copy-done
  2.1 1.3 %fusion.12 = bf16[2,7,7,256]{3,0,2,1:T(2,128)(2,1)S(1)} fusion(bf16[2,7,7,256]{3,0,2,1:T(2,128)(2,1)} %param.17, bf16[3,3,256,256]{3,2,1,0:T(8,128)(2,1)S(1)} %copy-done, f32[256]{0:T(256)} %param.26, f32[256]{0:T(256)} %param.23, bf16[2]{0:T(256)(128)(2,1)S(1)} %compare_convert_fusion), kind=kOutput, calls=%fused_computation.18 | convolution fusion | flops 94759424 | bytes 1282052 | tf_op jit(solution)/shard_map/conv_general_dilated | solution.py:21
  3.5 0.0 copy-start.2
  3.5 0.0 copy-start.4
  3.5 0.0 copy-start.8
  3.5 0.0 copy-start.9
  3.5 0.2 convolution_convert_fusion.2
  3.7 0.0 copy-done.6
  3.7 0.0 copy-done.7
  3.7 0.0 copy-done.3
  3.7 0.0 copy-done.5
  3.8 0.6 %fusion.8 = bf16[2,14,14,128]{3,0,2,1:T(2,128)(2,1)S(1)} fusion(bf16[2,14,14,128]{3,0,2,1:T(2,128)(2,1)S(1)} %copy-done.5, bf16[3,3,128,128]{3,2,1,0:T(8,128)(2,1)S(1)} %copy-done.3, f32[128]{0:T(128)S(1)} %copy-done.6, f32[128]{0:T(128)S(1)} %copy-done.7, bf16[2]{0:T(256)(128)(2,1)S(1)} %compare_convert_fusion), kind=kOutput, calls=%fused_computation.13 | convolution fusion | flops 105108480 | bytes 496644 | tf_op jit(solution)/shard_map/conv_general_dilated | solution.py:21
  4.4 0.2 convolution_convert_fusion.1
  4.6 0.0 copy-done.2
  4.6 0.0 copy-done.4
  4.6 0.0 copy-done.8
  4.6 0.0 copy-done.9
  4.7 1.9 %fusion.13 = bf16[2,28,28,64]{3,0,2,1:T(2,128)(2,1)S(1)} fusion(bf16[2,28,28,64]{3,0,2,1:T(2,128)(2,1)S(1)} %copy-done.2, bf16[3,3,64,64]{3,2,1,0:T(8,128)(2,1)S(1)} %copy-done.4, f32[64]{0:T(128)S(1)} %copy-done.8, f32[64]{0:T(128)S(1)} %copy-done.9, bf16[2]{0:T(256)(128)(2,1)S(1)} %compare_convert_fusion), kind=kOutput, calls=%fused_computation.20 | convolution fusion | flops 110667776 | bytes 475652 | tf_op jit(solution)/shard_map/conv_general_dilated | solution.py:21
  6.5 0.0 copy-start.1
  6.5 0.3 fusion.3
  6.8 0.1 pad.17.f1_ref
  6.9 1.1 %copy-done.1 = bf16[16,128,320]{2,1,0:T(8,128)(2,1)S(1)} copy-done((bf16[16,128,320]{2,1,0:T(8,128)(2,1)S(1)}, bf16[16,128,320]{2,1,0:T(8,128)(2,1)}, u32[]{:S(2)}) %copy-start.1) | copy-done | bytes 1310744
  7.9 49.6 %statistics.1 = (bf16[16,240,128]{2,1,0:T(8,128)(2,1)S(1)}, bf16[80,128]{1,0:T(8,128)(2,1)S(1)}) custom-call(bf16[2,29,32,128]{3,2,1,0:T(8,128)(2,1)S(1)} %pad.17.f1_ref, bf16[2,16,16,128]{3,2,1,0:T(8,128)(2,1)S(1)} %pad.18.f2_ref, bf16[2,8,16,128]{3,2,1,0:T(8,128)(2,1)S(1)} %pad.19.f3_ref, bf16[16,128,320]{2,1,0:T(8,128)(2,1)S(1)} %copy-done.1), custom_call_target="tpu_custom_call" | custom-call | flops 800000000 | bytes 4000000 | tf_op jit(solution)/shard_map/statistics/pallas_call | solution.py:299
  57.5 0.4 reshape.26
  58.0 0.7 %fusion.25 = f32[100,49]{0,1:T(8,128)} fusion(bf16[1,10240]{1,0:T(2,128)(2,1)S(1)} %bitcast.31, bf16[48,10240]{1,0:T(8,128)(2,1)S(1)} %reshape.26), kind=kLoop, calls=%fused_computation.34 | loop fusion | flops 44100 | bytes 1023120 | tf_op jit(solution)/shard_map/transpose | solution.py:337
  58.6 1.5 %fusion.7 = f32[49,10000]{1,0:T(8,128)} fusion(bf16[1,10240]{1,0:T(2,128)(2,1)S(1)} %bitcast.32, bf16[48,10240]{1,0:T(8,128)(2,1)S(1)} %reshape.26), kind=kLoop, calls=%fused_computation.12 | loop fusion | flops 1960000 | bytes 2963520 | tf_op jit(solution)/shard_map/convert_element_type | solution.py:332
  (5 shorter events, 0.1 us)
Async XLA Ops:
  0.6 1.5 %copy-start = (bf16[3,3,256,256]{3,2,1,0:T(8,128)(2,1)S(1)}, bf16[3,3,256,256]{3,2,1,0:T(8,128)(2,1)}, u32[]{:S(2)}) copy-start(bf16[3,3,256,256]{3,2,1,0:T(8,128)(2,1)} %param.20) | copy-start | bytes 3538948
  0.6 3.1 %copy-start.6 = (f32[128]{0:T(128)S(1)}, f32[128]{0:T(128)}, u32[]{:S(2)}) copy-start(f32[128]{0:T(128)} %param.25) | copy-start | bytes 1540
  0.7 3.1 %copy-start.7 = (f32[128]{0:T(128)S(1)}, f32[128]{0:T(128)}, u32[]{:S(2)}) copy-start(f32[128]{0:T(128)} %param.22) | copy-start | bytes 1540
  0.7 3.1 %copy-start.3 = (bf16[3,3,128,128]{3,2,1,0:T(8,128)(2,1)S(1)}, bf16[3,3,128,128]{3,2,1,0:T(8,128)(2,1)}, u32[]{:S(2)}) copy-start(bf16[3,3,128,128]{3,2,1,0:T(8,128)(2,1)} %param.19) | copy-start | bytes 884740
  0.7 3.1 %copy-start.5 = (bf16[2,14,14,128]{3,0,2,1:T(2,128)(2,1)S(1)}, bf16[2,14,14,128]{3,0,2,1:T(2,128)(2,1)}, u32[]{:S(2)}) copy-start(bf16[2,14,14,128]{3,0,2,1:T(2,128)(2,1)} %param.16) | copy-start | bytes 301060
  3.5 1.2 %copy-start.2 = (bf16[2,28,28,64]{3,0,2,1:T(2,128)(2,1)S(1)}, bf16[2,28,28,64]{3,0,2,1:T(2,128)(2,1)}, u32[]{:S(2)}) copy-start(bf16[2,28,28,64]{3,0,2,1:T(2,128)(2,1)} %param.15) | copy-start | bytes 602116
  3.5 1.1 %copy-start.4 = (bf16[3,3,64,64]{3,2,1,0:T(8,128)(2,1)S(1)}, bf16[3,3,64,64]{3,2,1,0:T(8,128)(2,1)}, u32[]{:S(2)}) copy-start(bf16[3,3,64,64]{3,2,1,0:T(8,128)(2,1)} %param.18) | copy-start | bytes 221188
  3.5 1.1 %copy-start.8 = (f32[64]{0:T(128)S(1)}, f32[64]{0:T(128)}, u32[]{:S(2)}) copy-start(f32[64]{0:T(128)} %param.24) | copy-start | bytes 772
  3.5 1.1 %copy-start.9 = (f32[64]{0:T(128)S(1)}, f32[64]{0:T(128)}, u32[]{:S(2)}) copy-start(f32[64]{0:T(128)} %param.21) | copy-start | bytes 772
  6.5 1.4 %copy-start.1 = (bf16[16,128,320]{2,1,0:T(8,128)(2,1)S(1)}, bf16[16,128,320]{2,1,0:T(8,128)(2,1)}, u32[]{:S(2)}) copy-start(bf16[16,128,320]{2,1,0:T(8,128)(2,1)} %constant.22.clone.table_ref) | copy-start | bytes 3932164

commit v2 on v1

v2 whole, which is shorter than its diff:
```python
import functools

import jax
import jax.numpy as jnp
import numpy as np
from jax import lax
from jax.experimental import pallas as pl
from jax.experimental.pallas import tpu as pltpu
from jax.sharding import PartitionSpec as P

MESH = pl.DeviceIdType.MESH
LANES = 128
ONES = 127
SLOTS = 4
WAVES = 2
PER_WAVE = SLOTS // WAVES
UNIT = 2 * PER_WAVE
FLAT = 80
WINDOW = 160


def section_out(images, weight, gain, bias):
    conv = lax.conv_general_dilated(
        images,
        weight,
        (1, 1),
        "SAME",
        dimension_numbers=("NHWC", "HWIO", "NHWC"),
        preferred_element_type=jnp.float32,
    )
    return jax.nn.relu(conv * gain + bias).astype(jnp.bfloat16)


def pick_channels(section, offset, slots):
    width = section.shape[3]
    table = (slots[None, :] - offset == lax.iota(jnp.int32, width)[:, None]).astype(jnp.bfloat16)
    return jnp.einsum(
        "ihwc,ck->ihwk", section, table, preferred_element_type=jnp.float32
    ).astype(jnp.bfloat16)


def gather_index(side, blocks, sharers):
    block = side * side // blocks
    own = block // sharers
    rows = sharers * UNIT
    index = np.full((WAVES * rows, LANES), -1, np.int32)
    for j in range(blocks):
        y0 = j * block // side
        for place in range(sharers):
            half, pair = divmod(place, sharers // 2)
            i = pair * 2 + (j + half) % 2
            for q in range(SLOTS):
                wave, part = divmod(q, PER_WAVE)
                position = j * block + (i * own + q if q < own else block - 1)
                y, x = divmod(position, side)
                columns = (
                    (y - y0) * 32 + x,
                    96 + (y // 2 - y0 // 2) * 16 + x // 2,
                    128 + (y // 4 - y0 // 4) * 16 + x // 4,
                )
                for g in range(2):
                    row = wave * rows + place * UNIT + g * PER_WAVE + part
                    index[row, j * 3 : j * 3 + 3] = columns
    return index


def iota(shape, dim):
    return lax.broadcasted_iota(jnp.int32, shape, dim)


def flatten_tables(kept):
    f = iota((FLAT, LANES), 0) * LANES
    k = iota((FLAT, LANES), 1)
    picks, masks = [], []
    start = jnp.floor((f.astype(jnp.float32) + 0.5) * (1.0 / kept))
    rest = f - start.astype(jnp.int32) * kept + k
    for t in range(3):
        picks.append(((k - t) * kept <= f) & (f < (k - t + 1) * kept))
        masks.append((rest >= t * kept) & (rest < (t + 1) * kept))
    return jnp.concatenate(picks, 0), masks


def packets(kept, gram, picks, masks, q):
    raw = gram[:, q * LANES : (q + 1) * LANES]
    k = iota((LANES, LANES), 0)
    eye = jnp.where(k == iota((LANES, LANES), 1), 0.01, 0.0)
    total = raw[ONES:, ONES:]
    mean = raw[ONES:, :] / total
    cov = (raw - raw[:, ONES:] * mean) / (total - 1.0) + eye
    for bit in (4, 8, 16, 32, 64):
        cov = jnp.where(((k * kept) & bit) != 0, pltpu.roll(cov, bit, 1), cov)
    flat = jnp.dot(picks, cov.astype(jnp.bfloat16), preferred_element_type=jnp.float32)
    packet = jnp.zeros((FLAT, LANES), jnp.float32)
    for t in range(3):
        packet = packet + jnp.where(masks[t], flat[t * FLAT : (t + 1) * FLAT], 0.0)
    row, lane = iota((FLAT, LANES), 0), iota((FLAT, LANES), 1)
    edge = kept * kept % LANES
    high = mean.astype(jnp.bfloat16).astype(jnp.float32)
    low = pltpu.roll(jnp.broadcast_to(mean - high, (8, LANES)), edge, 1)[:1]
    packet = jnp.where(row == FLAT - 1, high, packet)
    packet = jnp.where((row == FLAT - 2) & (lane >= edge), low, packet)
    return packet.astype(jnp.bfloat16)


def kernel(
    kept,
    f1_ref,
    f2_ref,
    f3_ref,
    index_hbm,
    out_ref,
    last_ref,
    index_ref,
    fetch_sem,
    s1_ref,
    s2_ref,
    r1_ref,
    r2_ref,
    x_ref,
    a_send,
    a_recv,
    b_send,
    b_recv,
    c_send,
    d_send,
    x_recv,
    z_send,
    z_recv,
    pair_send,
    pair_recv,
):
    groups, owners = r1_ref.shape[1], r2_ref.shape[1]
    chips = groups // 2
    me = lax.axis_index("img")
    pos = lax.axis_index("pos")
    z, core = me // 2, me % 2
    odd = (me + pos) % 2

    fetch = pltpu.make_async_copy(index_hbm, index_ref, fetch_sem)
    fetch.start()
    barrier = pltpu.get_barrier_semaphore()

    @pl.loop(1, groups)
    def _(d):
        pl.semaphore_signal(
            barrier, inc=1, device_id=(lax.rem(me + d, groups), pos), device_id_type=MESH
        )

    @pl.loop(1, owners)
    def _(d):
        pl.semaphore_signal(
            barrier, inc=1, device_id=(me, lax.rem(pos + d, owners)), device_id_type=MESH
        )

    fetch.wait()
    rows = WAVES * groups * UNIT
    column = iota((rows, WINDOW), 1)
    second = (iota((rows, LANES), 0) & PER_WAVE) != 0
    for j in range(owners):
        y0 = (7 * j) // 4
        halves = []
        for g in range(2):
            parts = []
            for ref, y, count in ((f1_ref, y0, 3), (f2_ref, y0 // 2, 2), (f3_ref, y0 // 4, 2)):
                parts.append(ref[g, y : y + count].reshape(-1, LANES))
            halves.append(jnp.concatenate(parts, 0))
        table = column == index_ref[:, 3 * j : 3 * j + 1]
        for t in (1, 2):
            table = table | (column == index_ref[:, 3 * j + t : 3 * j + t + 1])
        table = jnp.where(table, 1.0, 0.0).astype(jnp.bfloat16)
        both = jnp.dot(table, jnp.concatenate(halves, 1), preferred_element_type=jnp.float32)
        picked = jnp.where(second, both[:, LANES:], both[:, :LANES])
        picked = picked.reshape(WAVES, 2, groups // 2, UNIT, LANES).astype(jnp.bfloat16)
        for wave in range(WAVES):
            s1_ref[wave, :, j % 2, j // 2] = picked[wave, 0]
            s2_ref[wave, j] = picked[wave, 1]

    pl.semaphore_wait(barrier, groups - 1 + owners - 1)

    def remote(src, dst, send_sem, recv_sem, device):
        return pltpu.make_async_remote_copy(
            src_ref=src,
            dst_ref=dst,
            send_sem=send_sem,
            recv_sem=recv_sem,
            device_id=device,
            device_id_type=MESH,
        )

    def to_group(wave, d):
        to = lax.rem(me + d, groups)
        source = s1_ref.at[wave, to // 2, to % 2]
        sems = a_send.at[wave, d], a_recv.at[wave, d]
        return remote(source, r1_ref.at[wave, me], *sems, (to, pos))

    def to_owner(wave, d):
        to = lax.rem(pos + d, owners)
        sems = b_send.at[wave, d], b_recv.at[wave, d]
        return remote(s2_ref.at[wave, to], r2_ref.at[wave, pos], *sems, (me, to))

    def on_to_owner(wave, n):
        to = lax.rem(pos // 2 + n, owners // 2)
        sems = c_send.at[wave, n], x_recv.at[wave, pos]
        return remote(r1_ref.at[wave, :, to], x_ref.at[wave, pos], *sems, (me, 2 * to + core))

    def on_to_group(wave, n):
        to = lax.rem(z + n, chips)
        sems = d_send.at[wave, n], x_recv.at[wave, me]
        device = (2 * to + 1 - pos % 2, pos)
        return remote(r2_ref.at[wave, :, to], x_ref.at[wave, me], *sems, device)

    def far_first(n, count):
        return count // 2 + ((n + 1) // 2) * (1 - 2 * (n % 2))

    for wave in range(WAVES):

        @pl.loop(0, groups - 1)
        def _(n, wave=wave):
            to_group(wave, far_first(n, groups)).start()
            to_owner(wave, far_first(n, owners)).start()

    for wave in range(WAVES):
        r1_ref[wave, me] = s1_ref[wave, z, core]
        r2_ref[wave, pos] = s2_ref[wave, pos]
    tables = flatten_tables(kept)
    masks = tables[1]
    picks = jnp.where(tables[0], 1.0, 0.0).astype(jnp.bfloat16)

    for wave in range(WAVES):

        @pl.loop(1, owners)
        def _(d, wave=wave):
            to_owner(wave, d).wait()

        @pl.loop(odd, chips)
        def _(n, wave=wave):
            on_to_group(wave, n).start()

        @pl.loop(1, groups)
        def _(d, wave=wave):
            to_group(wave, d).wait()

        @pl.loop(1 - odd, owners // 2)
        def _(n, wave=wave):
            on_to_owner(wave, n).start()

    @pl.when(odd == 0)
    def _():
        for wave in range(WAVES):
            x_ref[wave, pos] = r1_ref[wave, :, pos // 2]

    @pl.when(odd == 1)
    def _():
        for wave in range(WAVES):
            x_ref[wave, me] = r2_ref[wave, :, z]

    mine = jnp.where(odd == 0, pos, me)

    def wave_gram(wave):
        @pl.loop(1, owners)
        def _(d):
            source = lax.rem(mine + d, owners)
            part = x_ref.at[wave, source]
            pltpu.make_async_copy(part, part, x_recv.at[wave, source]).wait()

        units = groups * owners
        x = x_ref[wave].astype(jnp.float32).reshape(units // 2, 2, UNIT, LANES)
        x = jnp.concatenate([x[:, 0], x[:, 1]], 1).reshape(units * UNIT, LANES)
        slot = iota((units * UNIT, LANES), 0) & (PER_WAVE - 1)
        spread = jnp.concatenate([jnp.where(slot == q, x, 0.0) for q in range(PER_WAVE)], 1)
        return lax.dot_general(
            x.astype(jnp.bfloat16),
            spread.astype(jnp.bfloat16),
            (((0,), (0,)), ((), ())),
            preferred_element_type=jnp.float32,
        )

    def device_at(distance):
        return (lax.rem(z + distance, chips) * 2 + core, pos)

    for q in range(SLOTS):
        if q % PER_WAVE == 0:
            gram = wave_gram(q // PER_WAVE)
        if q == SLOTS - 1:
            break
        rows = pl.ds(q * FLAT, FLAT)
        out_ref[me, rows] = packets(kept, gram, picks, masks, q % PER_WAVE)
        part = out_ref.at[me, rows]
        for distance in (4, 3, 5, 2, 6, 1, 7):
            sems = z_send.at[distance], z_recv.at[distance]
            remote(part, part, *sems, device_at(distance)).start()
    partner = (z * 2 + 1 - core, pos)

    def share(distance):
        part = out_ref.at[lax.rem(z + chips - distance, chips) * 2 + core]
        return remote(part, part, pair_send.at[distance], pair_recv.at[distance], partner)

    share(0).start()
    last_ref[...] = packets(kept, gram, picks, masks, PER_WAVE - 1)
    whole = out_ref.at[me]
    for distance in (1, 7, 2, 6, 3, 5, 4):
        sems = z_send.at[distance], z_recv.at[distance]
        remote(whole, whole, *sems, device_at(distance)).wait_recv()
        share(distance).start()
    for distance in range(1, chips):
        sems = z_send.at[distance], z_recv.at[distance]
        remote(whole, whole, *sems, device_at(distance)).wait_send()

    for wave in range(WAVES):

        @pl.loop(odd, chips)
        def _(n, wave=wave):
            on_to_group(wave, n).wait_send()

        @pl.loop(1 - odd, owners // 2)
        def _(n, wave=wave):
            on_to_owner(wave, n).wait_send()

    for distance in range(chips):
        share(distance).wait()


def per_device(
    section_one,
    section_two,
    section_three,
    weight_one,
    weight_two,
    weight_three,
    gain_one,
    gain_two,
    gain_three,
    bias_one,
    bias_two,
    bias_three,
    channel_index,
    valid_count,
):
    images, side = section_one.shape[:2]
    width_one, width_two = section_one.shape[3], section_two.shape[3]
    kept = channel_index.shape[0]
    groups, owners = lax.axis_size("img"), lax.axis_size("pos")
    block = side * side // owners
    scale = (lax.iota(jnp.int32, images) < valid_count[0, 0]).astype(jnp.bfloat16)
    scale = scale[:, None, None, None]
    out_one = section_out(section_one, weight_one, gain_one, bias_one) * scale
    out_two = section_out(section_two, weight_two, gain_two, bias_two) * scale
    out_three = section_out(section_three, weight_three, gain_three, bias_three) * scale
    slots = jnp.pad(channel_index, (0, LANES - kept), constant_values=-1024)
    f1 = pick_channels(out_one, 0, slots)
    f1 = jnp.where(lax.iota(jnp.int32, LANES) == ONES, scale, f1)
    f2 = pick_channels(out_two, width_one, slots)
    f3 = pick_channels(out_three, width_one + width_two, slots)
    f1 = jnp.pad(f1, ((0, 0), (0, 1), (0, 4), (0, 0)))
    f2 = jnp.pad(f2, ((0, 0), (0, 2), (0, 2), (0, 0)))
    f3 = jnp.pad(f3, ((0, 0), (0, 1), (0, 9), (0, 0)))
    index = jnp.asarray(gather_index(side, owners, groups))
    own = SLOTS - 1
    vmem = pl.BlockSpec(memory_space=pltpu.VMEM)
    dma = pltpu.SemaphoreType.DMA
    out, last = pl.pallas_call(
        functools.partial(kernel, kept),
        out_shape=(
            jax.ShapeDtypeStruct((groups, own * FLAT, LANES), jnp.bfloat16),
            jax.ShapeDtypeStruct((FLAT, LANES), jnp.bfloat16),
        ),
        in_specs=[vmem] * 3 + [pl.BlockSpec(memory_space=pl.ANY)],
        out_specs=[vmem] * 2,
        scratch_shapes=[
            pltpu.VMEM(index.shape, jnp.int32),
            dma(()),
            pltpu.VMEM((WAVES, groups // 2, 2, owners // 2, UNIT, LANES), jnp.bfloat16),
            pltpu.VMEM((WAVES, owners, groups // 2, UNIT, LANES), jnp.bfloat16),
            pltpu.VMEM((WAVES, groups, owners // 2, UNIT, LANES), jnp.bfloat16),
            pltpu.VMEM((WAVES, owners, groups // 2, UNIT, LANES), jnp.bfloat16),
            pltpu.VMEM((WAVES, owners, groups, UNIT, LANES), jnp.bfloat16),
            dma((WAVES, groups)),
            dma((WAVES, groups)),
            dma((WAVES, owners)),
            dma((WAVES, owners)),
            dma((WAVES, owners // 2)),
            dma((WAVES, groups // 2)),
            dma((WAVES, owners)),
            dma((groups // 2,)),
            dma((groups // 2,)),
            dma((groups // 2,)),
            dma((groups // 2,)),
        ],
        compiler_params=pltpu.CompilerParams(
            collective_id=0, has_side_effects=True, vmem_limit_bytes=40 * 2**20
        ),
        cost_estimate=pl.CostEstimate(
            flops=800_000_000, bytes_accessed=4_000_000, transcendentals=0
        ),
        name="statistics",
    )(f1, f2, f3, index)
    packets = jnp.concatenate(
        [out.reshape(block - 1, FLAT * LANES), last.reshape(1, FLAT * LANES)]
    ).astype(jnp.float32)
    used = kept * kept
    covariance = packets[:, :used]
    end = (FLAT - 1) * LANES
    mean = packets[:, end : end + kept] + packets[:, used : used + kept]
    return (mean.T, covariance)


def solution(mesh):
    return jax.shard_map(
        per_device,
        mesh=mesh,
        in_specs=(P(("img", "pos"), None, None, None),) * 3
        + (P(),) * 10
        + (P("img", "pos"),),
        out_specs=(P(None, "pos"), P("pos", None)),
        check_vma=False,
    )
```

time: 60.4 us -> 50.9 us (0.84)
  Pallas kernels: 49.6 us -> 40.6 us
    pallas_call x1, Pallas kernels: 49.6 us -> 40.6 us  [per_device(): pl.pallas_call(functools.partial(kernel, kept), out_shape=(jax.ShapeDtype...]
where the time goes in v2:
time: 50.9 us; the launch traced here: 50.7 us
  Pallas kernels  40.6 us (80%)
  matrix products  4.45 us (9%)
  other arithmetic  2.89 us (6%)
  between operations  1.64 us (3%)
  local copies, waits for them, and re-layouts  1.09 us (2%)
    pallas_call x1, Pallas kernels, per_device(): pl.pallas_call(functools.partial(kernel, kept), out_shape=(jax.ShapeDtype...  40.6 us
    conv_general_dilated x3, matrix products, section_out(): lax.conv_general_dilated(images, weight, (1, 1), 'SAME', dimension_number...  3.85 us
    convert_element_type x1, other arithmetic, per_device(): packets = jnp.concatenate([out.reshape(block - 1, FLAT * LANES), last.res...  1.53 us

profile of v2, /device:TPU:1, one launch (start us, length us, event | category | flops | bytes accessed | tf_op | source)
XLA Modules:
  0.0 50.7 jit_solution(15926464884985041002)
XLA Ops:
  0.6 0.0 copy-start
  0.6 0.0 copy-start.6
  0.7 0.0 copy-start.7
  0.7 0.0 copy-start.3
  0.7 0.0 copy-start.5
  1.5 0.7 %broadcast_add_fusion = (s32[128]{0:T(128)S(1)}, s32[128]{0:T(128)S(1)}, s32[128]{0:T(128)S(1)}) fusion(s32[100]{0:T(128)} %param.27), kind=kLoop, calls=%fused_computation.38 | loop fusion | flops 256 | bytes 1936 | tf_op jit(solution)/shard_map/sub | solution.py:36
  2.1 0.0 copy-done
  2.1 1.3 %fusion.12 = bf16[2,7,7,256]{3,0,2,1:T(2,128)(2,1)S(1)} fusion(bf16[2,7,7,256]{3,0,2,1:T(2,128)(2,1)} %param.17, bf16[3,3,256,256]{3,2,1,0:T(8,128)(2,1)S(1)} %copy-done, f32[256]{0:T(256)} %param.26, f32[256]{0:T(256)} %param.23, bf16[2]{0:T(256)(128)(2,1)S(1)} %compare_convert_fusion), kind=kOutput, calls=%fused_computation.18 | convolution fusion | flops 94759424 | bytes 1282052 | tf_op jit(solution)/shard_map/conv_general_dilated | solution.py:23
  3.5 0.0 copy-start.2
  3.5 0.0 copy-start.4
  3.5 0.0 copy-start.8
  3.5 0.0 copy-start.9
  3.5 0.2 convolution_convert_fusion.2
  3.7 0.0 copy-done.6
  3.7 0.0 copy-done.7
  3.7 0.0 copy-done.3
  3.7 0.0 copy-done.5
  3.8 0.7 %fusion.8 = bf16[2,14,14,128]{3,0,2,1:T(2,128)(2,1)S(1)} fusion(bf16[2,14,14,128]{3,0,2,1:T(2,128)(2,1)S(1)} %copy-done.5, bf16[3,3,128,128]{3,2,1,0:T(8,128)(2,1)S(1)} %copy-done.3, f32[128]{0:T(128)S(1)} %copy-done.6, f32[128]{0:T(128)S(1)} %copy-done.7, bf16[2]{0:T(256)(128)(2,1)S(1)} %compare_convert_fusion), kind=kOutput, calls=%fused_computation.13 | convolution fusion | flops 105108480 | bytes 496644 | tf_op jit(solution)/shard_map/conv_general_dilated | solution.py:23
  4.4 0.2 convolution_convert_fusion.1
  4.6 0.0 copy-done.2
  4.6 0.0 copy-done.4
  4.7 0.0 copy-done.8
  4.7 0.0 copy-done.9
  4.7 1.9 %fusion.13 = bf16[2,28,28,64]{3,0,2,1:T(2,128)(2,1)S(1)} fusion(bf16[2,28,28,64]{3,0,2,1:T(2,128)(2,1)S(1)} %copy-done.2, bf16[3,3,64,64]{3,2,1,0:T(8,128)(2,1)S(1)} %copy-done.4, f32[64]{0:T(128)S(1)} %copy-done.8, f32[64]{0:T(128)S(1)} %copy-done.9, bf16[2]{0:T(256)(128)(2,1)S(1)} %compare_convert_fusion), kind=kOutput, calls=%fused_computation.20 | convolution fusion | flops 110667776 | bytes 475652 | tf_op jit(solution)/shard_map/conv_general_dilated | solution.py:23
  6.5 0.0 copy-start.1
  6.5 0.3 fusion.3
  6.8 0.1 pad.17.f1_ref
  6.9 0.5 copy-done.1
  7.4 40.6 %statistics.1 = (bf16[16,240,128]{2,1,0:T(8,128)(2,1)S(1)}, bf16[80,128]{1,0:T(8,128)(2,1)S(1)}) custom-call(bf16[2,29,32,128]{3,2,1,0:T(8,128)(2,1)S(1)} %pad.17.f1_ref, bf16[2,16,16,128]{3,2,1,0:T(8,128)(2,1)S(1)} %pad.18.f2_ref, bf16[2,8,16,128]{3,2,1,0:T(8,128)(2,1)S(1)} %pad.19.f3_ref, s32[128,128]{1,0:T(8,128)S(1)} %copy-done.1), custom_call_target="tpu_custom_call" | custom-call | flops 800000000 | bytes 4000000 | tf_op jit(solution)/shard_map/statistics/pallas_call | solution.py:361
  48.0 0.4 reshape.26
  48.5 0.7 %fusion.25 = f32[100,49]{0,1:T(8,128)} fusion(bf16[1,10240]{1,0:T(2,128)(2,1)S(1)} %bitcast.31, bf16[48,10240]{1,0:T(8,128)(2,1)S(1)} %reshape.26), kind=kLoop, calls=%fused_computation.34 | loop fusion | flops 44100 | bytes 1023120 | tf_op jit(solution)/shard_map/transpose | solution.py:404
  49.2 1.5 %fusion.7 = f32[49,10000]{1,0:T(8,128)} fusion(bf16[1,10240]{1,0:T(2,128)(2,1)S(1)} %bitcast.32, bf16[48,10240]{1,0:T(8,128)(2,1)S(1)} %reshape.26), kind=kLoop, calls=%fused_computation.12 | loop fusion | flops 1960000 | bytes 2963520 | tf_op jit(solution)/shard_map/convert_element_type | solution.py:399
  (5 shorter events, 0.1 us)
Async XLA Ops:
  0.6 1.5 %copy-start = (bf16[3,3,256,256]{3,2,1,0:T(8,128)(2,1)S(1)}, bf16[3,3,256,256]{3,2,1,0:T(8,128)(2,1)}, u32[]{:S(2)}) copy-start(bf16[3,3,256,256]{3,2,1,0:T(8,128)(2,1)} %param.20) | copy-start | bytes 3538948
  0.6 3.1 %copy-start.6 = (f32[128]{0:T(128)S(1)}, f32[128]{0:T(128)}, u32[]{:S(2)}) copy-start(f32[128]{0:T(128)} %param.25) | copy-start | bytes 1540
  0.7 3.1 %copy-start.7 = (f32[128]{0:T(128)S(1)}, f32[128]{0:T(128)}, u32[]{:S(2)}) copy-start(f32[128]{0:T(128)} %param.22) | copy-start | bytes 1540
  0.7 3.1 %copy-start.3 = (bf16[3,3,128,128]{3,2,1,0:T(8,128)(2,1)S(1)}, bf16[3,3,128,128]{3,2,1,0:T(8,128)(2,1)}, u32[]{:S(2)}) copy-start(bf16[3,3,128,128]{3,2,1,0:T(8,128)(2,1)} %param.19) | copy-start | bytes 884740
  0.7 3.1 %copy-start.5 = (bf16[2,14,14,128]{3,0,2,1:T(2,128)(2,1)S(1)}, bf16[2,14,14,128]{3,0,2,1:T(2,128)(2,1)}, u32[]{:S(2)}) copy-start(bf16[2,14,14,128]{3,0,2,1:T(2,128)(2,1)} %param.16) | copy-start | bytes 301060
  3.5 1.2 %copy-start.2 = (bf16[2,28,28,64]{3,0,2,1:T(2,128)(2,1)S(1)}, bf16[2,28,28,64]{3,0,2,1:T(2,128)(2,1)}, u32[]{:S(2)}) copy-start(bf16[2,28,28,64]{3,0,2,1:T(2,128)(2,1)} %param.15) | copy-start | bytes 602116
  3.5 1.2 %copy-start.4 = (bf16[3,3,64,64]{3,2,1,0:T(8,128)(2,1)S(1)}, bf16[3,3,64,64]{3,2,1,0:T(8,128)(2,1)}, u32[]{:S(2)}) copy-start(bf16[3,3,64,64]{3,2,1,0:T(8,128)(2,1)} %param.18) | copy-start | bytes 221188
  3.5 1.2 %copy-start.8 = (f32[64]{0:T(128)S(1)}, f32[64]{0:T(128)}, u32[]{:S(2)}) copy-start(f32[64]{0:T(128)} %param.24) | copy-start | bytes 772
  3.5 1.2 %copy-start.9 = (f32[64]{0:T(128)S(1)}, f32[64]{0:T(128)}, u32[]{:S(2)}) copy-start(f32[64]{0:T(128)} %param.21) | copy-start | bytes 772
  6.5 0.8 %copy-start.1 = (s32[128,128]{1,0:T(8,128)S(1)}, s32[128,128]{1,0:T(8,128)}, u32[]{:S(2)}) copy-start(s32[128,128]{1,0:T(8,128)} %constant.22.clone.index_hbm) | copy-start | bytes 196612

commit v3 on v2

--- a/solution.py
+++ b/solution.py
@@ -17,6 +17,9 @@
 UNIT = 2 * PER_WAVE
 FLAT = 80
 WINDOW = 160
+WHOLE = ((0, 2 * FLAT), (2 * FLAT, FLAT))
+LOWER = ((0, FLAT), (2 * FLAT, 32))
+UPPER = ((FLAT, FLAT), (2 * FLAT + 32, FLAT - 32))
 
 
 def section_out(images, weight, gain, bias):
@@ -111,7 +114,7 @@
     out_ref,
     last_ref,
     index_ref,
-    fetch_sem,
+    index_sem,
     s1_ref,
     s2_ref,
     r1_ref,
@@ -136,7 +139,7 @@
     z, core = me // 2, me % 2
     odd = (me + pos) % 2
 
-    fetch = pltpu.make_async_copy(index_hbm, index_ref, fetch_sem)
+    fetch = pltpu.make_async_copy(index_hbm, index_ref, index_sem)
     fetch.start()
     barrier = pltpu.get_barrier_semaphore()
 
@@ -152,30 +155,34 @@
             barrier, inc=1, device_id=(me, lax.rem(pos + d, owners)), device_id_type=MESH
         )
 
+    rows = groups * UNIT
+    second = (iota((rows, LANES), 0) & PER_WAVE) != 0
+
+    column = iota((rows, WINDOW), 1)
     fetch.wait()
-    rows = WAVES * groups * UNIT
-    column = iota((rows, WINDOW), 1)
-    second = (iota((rows, LANES), 0) & PER_WAVE) != 0
-    for j in range(owners):
-        y0 = (7 * j) // 4
-        halves = []
-        for g in range(2):
-            parts = []
-            for ref, y, count in ((f1_ref, y0, 3), (f2_ref, y0 // 2, 2), (f3_ref, y0 // 4, 2)):
-                parts.append(ref[g, y : y + count].reshape(-1, LANES))
-            halves.append(jnp.concatenate(parts, 0))
-        table = column == index_ref[:, 3 * j : 3 * j + 1]
-        for t in (1, 2):
-            table = table | (column == index_ref[:, 3 * j + t : 3 * j + t + 1])
-        table = jnp.where(table, 1.0, 0.0).astype(jnp.bfloat16)
-        both = jnp.dot(table, jnp.concatenate(halves, 1), preferred_element_type=jnp.float32)
-        picked = jnp.where(second, both[:, LANES:], both[:, :LANES])
-        picked = picked.reshape(WAVES, 2, groups // 2, UNIT, LANES).astype(jnp.bfloat16)
-        for wave in range(WAVES):
-            s1_ref[wave, :, j % 2, j // 2] = picked[wave, 0]
-            s2_ref[wave, j] = picked[wave, 1]
-
-    pl.semaphore_wait(barrier, groups - 1 + owners - 1)
+
+    def gather(wave):
+        for j in range(owners):
+            table = False
+            for t in range(3):
+                at = index_ref[wave * rows : (wave + 1) * rows, 3 * j + t : 3 * j + t + 1]
+                table = table | (column == at)
+            y0 = (7 * j) // 4
+            halves = []
+            for g in range(2):
+                parts = []
+                for ref, y, count in ((f1_ref, y0, 3), (f2_ref, y0 // 2, 2), (f3_ref, y0 // 4, 2)):
+                    parts.append(ref[g, y : y + count].reshape(-1, LANES))
+                halves.append(jnp.concatenate(parts, 0))
+            both = jnp.dot(
+                jnp.where(table, 1.0, 0.0).astype(jnp.bfloat16),
+                jnp.concatenate(halves, 1),
+                preferred_element_type=jnp.float32,
+            )
+            picked = jnp.where(second, both[:, LANES:], both[:, :LANES])
+            picked = picked.reshape(2, groups // 2, UNIT, LANES).astype(jnp.bfloat16)
+            s1_ref[wave, :, j % 2, j // 2] = picked[0]
+            s2_ref[wave, j] = picked[1]
 
     def remote(src, dst, send_sem, recv_sem, device):
         return pltpu.make_async_remote_copy(
@@ -213,10 +220,16 @@
         return count // 2 + ((n + 1) // 2) * (1 - 2 * (n % 2))
 
     for wave in range(WAVES):
+        gather(wave)
+        if wave == 0:
+            pl.semaphore_wait(barrier, groups - 1 + owners - 1)
 
         @pl.loop(0, groups - 1)
         def _(n, wave=wave):
             to_group(wave, far_first(n, groups)).start()
+
+        @pl.loop(0, owners - 1)
+        def _(n, wave=wave):
             to_owner(wave, far_first(n, owners)).start()
 
     for wave in range(WAVES):
@@ -275,36 +288,62 @@
             preferred_element_type=jnp.float32,
         )
 
-    def device_at(distance):
-        return (lax.rem(z + distance, chips) * 2 + core, pos)
-
-    for q in range(SLOTS):
+    def slot_at(distance):
+        return lax.rem(z + chips - distance, chips) * 2 + core
+
+    def share(rows, origin, target, sems, send, came):
+        part = out_ref.at[slot_at(origin), pl.ds(*rows)]
+        device = (lax.rem(z + target, chips) * 2 + core, pos)
+        return remote(part, part, z_send.at[sems, send], z_recv.at[sems, came], device)
+
+    def pair(wave, origin):
+        part = out_ref.at[slot_at(origin), pl.ds(*WHOLE[wave])]
+        sems = pair_send.at[wave, origin], pair_recv.at[wave, origin]
+        return remote(part, part, *sems, (z * 2 + 1 - core, pos))
+
+    sent = []
+
+    def begin(wave):
+        for target in (2, 6, 1, 7):
+            sent.append(share(WHOLE[wave], 0, target, wave, target, target))
+            sent[-1].start()
+
+    def arrive(wave, origin):
+        if origin == 4:
+            share(LOWER[wave], 4, 1, wave, 0, 4).wait_recv()
+            share(UPPER[wave], 4, 1, wave, 0, 0).wait_recv()
+        else:
+            share(WHOLE[wave], origin, 1, wave, 0, origin).wait_recv()
+        if origin == 2:
+            sent.append(share(LOWER[wave], 2, 2, wave, 4, 4))
+            sent.append(share(WHOLE[wave], 2, 1, wave, 3, 3))
+        elif origin == 6:
+            sent.append(share(UPPER[wave], 6, 6, wave, 0, 0))
+            sent.append(share(WHOLE[wave], 6, 7, wave, 5, 5))
+        if origin in (2, 6):
+            sent[-2].start()
+            sent[-1].start()
+        pair(wave, origin).start()
+
+    for q in range(SLOTS - 1):
         if q % PER_WAVE == 0:
             gram = wave_gram(q // PER_WAVE)
-        if q == SLOTS - 1:
-            break
         rows = pl.ds(q * FLAT, FLAT)
         out_ref[me, rows] = packets(kept, gram, picks, masks, q % PER_WAVE)
-        part = out_ref.at[me, rows]
-        for distance in (4, 3, 5, 2, 6, 1, 7):
-            sems = z_send.at[distance], z_recv.at[distance]
-            remote(part, part, *sems, device_at(distance)).start()
-    partner = (z * 2 + 1 - core, pos)
-
-    def share(distance):
-        part = out_ref.at[lax.rem(z + chips - distance, chips) * 2 + core]
-        return remote(part, part, pair_send.at[distance], pair_recv.at[distance], partner)
-
-    share(0).start()
+        if q == PER_WAVE - 1:
+            begin(0)
+            pair(0, 0).start()
+    begin(1)
+    pair(1, 0).start()
     last_ref[...] = packets(kept, gram, picks, masks, PER_WAVE - 1)
-    whole = out_ref.at[me]
-    for distance in (1, 7, 2, 6, 3, 5, 4):
-        sems = z_send.at[distance], z_recv.at[distance]
-        remote(whole, whole, *sems, device_at(distance)).wait_recv()
-        share(distance).start()
-    for distance in range(1, chips):
-        sems = z_send.at[distance], z_recv.at[distance]
-        remote(whole, whole, *sems, device_at(distance)).wait_send()
+    for wave in range(WAVES):
+        for origin in (2, 6, 1, 7):
+            arrive(wave, origin)
+    for wave in range(WAVES):
+        for origin in (3, 5, 4):
+            arrive(wave, origin)
+    for copy in sent:
+        copy.wait_send()
 
     for wave in range(WAVES):
 
@@ -316,8 +355,9 @@
         def _(n, wave=wave):
             on_to_owner(wave, n).wait_send()
 
-    for distance in range(chips):
-        share(distance).wait()
+    for wave in range(WAVES):
+        for origin in range(chips):
+            pair(wave, origin).wait()
 
 
 def per_device(
@@ -364,7 +404,7 @@
             jax.ShapeDtypeStruct((groups, own * FLAT, LANES), jnp.bfloat16),
             jax.ShapeDtypeStruct((FLAT, LANES), jnp.bfloat16),
         ),
-        in_specs=[vmem] * 3 + [pl.BlockSpec(memory_space=pl.ANY)],
+        in_specs=[vmem] * 3 + [pl.BlockSpec(memory_space=pltpu.HBM)],
         out_specs=[vmem] * 2,
         scratch_shapes=[
             pltpu.VMEM(index.shape, jnp.int32),
@@ -381,10 +421,10 @@
             dma((WAVES, owners // 2)),
             dma((WAVES, groups // 2)),
             dma((WAVES, owners)),
-            dma((groups // 2,)),
-            dma((groups // 2,)),
-            dma((groups // 2,)),
-            dma((groups // 2,)),
+            dma((WAVES, groups // 2)),
+            dma((WAVES, groups // 2)),
+            dma((WAVES, groups // 2)),
+            dma((WAVES, groups // 2)),
         ],
         compiler_params=pltpu.CompilerParams(
             collective_id=0, has_side_effects=True, vmem_limit_bytes=40 * 2**20

time: 50.9 us -> 47.7 us (0.937)
  Pallas kernels: 40.6 us -> 37.4 us
    pallas_call x1, Pallas kernels: 40.6 us -> 37.4 us  [per_device(): pl.pallas_call(functools.partial(kernel, kept), out_shape=(jax.ShapeDtype...]
where the time goes in v3:
time: 47.7 us; the launch traced here: 47.5 us
  Pallas kernels  37.4 us (78%)
  matrix products  4.45 us (9%)
  other arithmetic  2.89 us (6%)
  between operations  1.64 us (3%)
  local copies, waits for them, and re-layouts  1.09 us (2%)
    pallas_call x1, Pallas kernels, per_device(): pl.pallas_call(functools.partial(kernel, kept), out_shape=(jax.ShapeDtype...  37.4 us
    conv_general_dilated x3, matrix products, section_out(): lax.conv_general_dilated(images, weight, (1, 1), 'SAME', dimension_number...  3.85 us
    convert_element_type x1, other arithmetic, per_device(): packets = jnp.concatenate([out.reshape(block - 1, FLAT * LANES), last.res...  1.53 us

profile of v3, /device:TPU:1, one launch (start us, length us, event | category | flops | bytes accessed | tf_op | source)
XLA Modules:
  0.0 47.5 jit_solution(2958696067786073295)
XLA Ops:
  0.6 0.0 copy-start
  0.6 0.0 copy-start.6
  0.7 0.0 copy-start.7
  0.7 0.0 copy-start.3
  0.7 0.0 copy-start.5
  1.5 0.7 %broadcast_add_fusion = (s32[128]{0:T(128)S(1)}, s32[128]{0:T(128)S(1)}, s32[128]{0:T(128)S(1)}) fusion(s32[100]{0:T(128)} %param.27), kind=kLoop, calls=%fused_computation.38 | loop fusion | flops 256 | bytes 1936 | tf_op jit(solution)/shard_map/sub | solution.py:39
  2.1 0.0 copy-done
  2.1 1.3 %fusion.12 = bf16[2,7,7,256]{3,0,2,1:T(2,128)(2,1)S(1)} fusion(bf16[2,7,7,256]{3,0,2,1:T(2,128)(2,1)} %param.17, bf16[3,3,256,256]{3,2,1,0:T(8,128)(2,1)S(1)} %copy-done, f32[256]{0:T(256)} %param.26, f32[256]{0:T(256)} %param.23, bf16[2]{0:T(256)(128)(2,1)S(1)} %compare_convert_fusion), kind=kOutput, calls=%fused_computation.18 | convolution fusion | flops 94759424 | bytes 1282052 | tf_op jit(solution)/shard_map/conv_general_dilated | solution.py:26
  3.5 0.0 copy-start.2
  3.5 0.0 copy-start.4
  3.5 0.0 copy-start.8
  3.5 0.0 copy-start.9
  3.5 0.2 convolution_convert_fusion.2
  3.7 0.0 copy-done.6
  3.7 0.0 copy-done.7
  3.7 0.0 copy-done.3
  3.7 0.0 copy-done.5
  3.8 0.7 %fusion.8 = bf16[2,14,14,128]{3,0,2,1:T(2,128)(2,1)S(1)} fusion(bf16[2,14,14,128]{3,0,2,1:T(2,128)(2,1)S(1)} %copy-done.5, bf16[3,3,128,128]{3,2,1,0:T(8,128)(2,1)S(1)} %copy-done.3, f32[128]{0:T(128)S(1)} %copy-done.6, f32[128]{0:T(128)S(1)} %copy-done.7, bf16[2]{0:T(256)(128)(2,1)S(1)} %compare_convert_fusion), kind=kOutput, calls=%fused_computation.13 | convolution fusion | flops 105108480 | bytes 496644 | tf_op jit(solution)/shard_map/conv_general_dilated | solution.py:26
  4.4 0.2 convolution_convert_fusion.1
  4.6 0.0 copy-done.2
  4.6 0.0 copy-done.4
  4.7 0.0 copy-done.8
  4.7 0.0 copy-done.9
  4.7 1.9 %fusion.13 = bf16[2,28,28,64]{3,0,2,1:T(2,128)(2,1)S(1)} fusion(bf16[2,28,28,64]{3,0,2,1:T(2,128)(2,1)S(1)} %copy-done.2, bf16[3,3,64,64]{3,2,1,0:T(8,128)(2,1)S(1)} %copy-done.4, f32[64]{0:T(128)S(1)} %copy-done.8, f32[64]{0:T(128)S(1)} %copy-done.9, bf16[2]{0:T(256)(128)(2,1)S(1)} %compare_convert_fusion), kind=kOutput, calls=%fused_computation.20 | convolution fusion | flops 110667776 | bytes 475652 | tf_op jit(solution)/shard_map/conv_general_dilated | solution.py:26
  6.5 0.0 copy-start.1
  6.5 0.3 fusion.3
  6.8 0.1 pad.17.f1_ref
  6.9 0.5 %copy-done.1 = s32[128,128]{1,0:T(8,128)S(1)} copy-done((s32[128,128]{1,0:T(8,128)S(1)}, s32[128,128]{1,0:T(8,128)}, u32[]{:S(2)}) %copy-start.1) | copy-done | bytes 65560
  7.4 37.4 %statistics.1 = (bf16[16,240,128]{2,1,0:T(8,128)(2,1)S(1)}, bf16[80,128]{1,0:T(8,128)(2,1)S(1)}) custom-call(bf16[2,29,32,128]{3,2,1,0:T(8,128)(2,1)S(1)} %pad.17.f1_ref, bf16[2,16,16,128]{3,2,1,0:T(8,128)(2,1)S(1)} %pad.18.f2_ref, bf16[2,8,16,128]{3,2,1,0:T(8,128)(2,1)S(1)} %pad.19.f3_ref, s32[128,128]{1,0:T(8,128)S(1)} %copy-done.1), custom_call_target="tpu_custom_call" | custom-call | flops 800000000 | bytes 4000000 | tf_op jit(solution)/shard_map/statistics/pallas_call | solution.py:401
  44.8 0.4 reshape.26
  45.3 0.7 %fusion.25 = f32[100,49]{0,1:T(8,128)} fusion(bf16[1,10240]{1,0:T(2,128)(2,1)S(1)} %bitcast.31, bf16[48,10240]{1,0:T(8,128)(2,1)S(1)} %reshape.26), kind=kLoop, calls=%fused_computation.34 | loop fusion | flops 44100 | bytes 1023120 | tf_op jit(solution)/shard_map/transpose | solution.py:444
  45.9 1.5 %fusion.7 = f32[49,10000]{1,0:T(8,128)} fusion(bf16[1,10240]{1,0:T(2,128)(2,1)S(1)} %bitcast.32, bf16[48,10240]{1,0:T(8,128)(2,1)S(1)} %reshape.26), kind=kLoop, calls=%fused_computation.12 | loop fusion | flops 1960000 | bytes 2963520 | tf_op jit(solution)/shard_map/convert_element_type | solution.py:439
  (5 shorter events, 0.1 us)
Async XLA Ops:
  0.6 1.5 %copy-start = (bf16[3,3,256,256]{3,2,1,0:T(8,128)(2,1)S(1)}, bf16[3,3,256,256]{3,2,1,0:T(8,128)(2,1)}, u32[]{:S(2)}) copy-start(bf16[3,3,256,256]{3,2,1,0:T(8,128)(2,1)} %param.20) | copy-start | bytes 3538948
  0.6 3.1 %copy-start.6 = (f32[128]{0:T(128)S(1)}, f32[128]{0:T(128)}, u32[]{:S(2)}) copy-start(f32[128]{0:T(128)} %param.25) | copy-start | bytes 1540
  0.7 3.1 %copy-start.7 = (f32[128]{0:T(128)S(1)}, f32[128]{0:T(128)}, u32[]{:S(2)}) copy-start(f32[128]{0:T(128)} %param.22) | copy-start | bytes 1540
  0.7 3.1 %copy-start.3 = (bf16[3,3,128,128]{3,2,1,0:T(8,128)(2,1)S(1)}, bf16[3,3,128,128]{3,2,1,0:T(8,128)(2,1)}, u32[]{:S(2)}) copy-start(bf16[3,3,128,128]{3,2,1,0:T(8,128)(2,1)} %param.19) | copy-start | bytes 884740
  0.7 3.1 %copy-start.5 = (bf16[2,14,14,128]{3,0,2,1:T(2,128)(2,1)S(1)}, bf16[2,14,14,128]{3,0,2,1:T(2,128)(2,1)}, u32[]{:S(2)}) copy-start(bf16[2,14,14,128]{3,0,2,1:T(2,128)(2,1)} %param.16) | copy-start | bytes 301060
  3.5 1.2 %copy-start.2 = (bf16[2,28,28,64]{3,0,2,1:T(2,128)(2,1)S(1)}, bf16[2,28,28,64]{3,0,2,1:T(2,128)(2,1)}, u32[]{:S(2)}) copy-start(bf16[2,28,28,64]{3,0,2,1:T(2,128)(2,1)} %param.15) | copy-start | bytes 602116
  3.5 1.2 %copy-start.4 = (bf16[3,3,64,64]{3,2,1,0:T(8,128)(2,1)S(1)}, bf16[3,3,64,64]{3,2,1,0:T(8,128)(2,1)}, u32[]{:S(2)}) copy-start(bf16[3,3,64,64]{3,2,1,0:T(8,128)(2,1)} %param.18) | copy-start | bytes 221188
  3.5 1.2 %copy-start.8 = (f32[64]{0:T(128)S(1)}, f32[64]{0:T(128)}, u32[]{:S(2)}) copy-start(f32[64]{0:T(128)} %param.24) | copy-start | bytes 772
  3.5 1.2 %copy-start.9 = (f32[64]{0:T(128)S(1)}, f32[64]{0:T(128)}, u32[]{:S(2)}) copy-start(f32[64]{0:T(128)} %param.21) | copy-start | bytes 772
  6.5 0.8 %copy-start.1 = (s32[128,128]{1,0:T(8,128)S(1)}, s32[128,128]{1,0:T(8,128)}, u32[]{:S(2)}) copy-start(s32[128,128]{1,0:T(8,128)} %constant.22.clone.index_hbm) | copy-start | bytes 196612

commit v4 on v3

--- a/solution.py
+++ b/solution.py
@@ -124,8 +124,7 @@
     a_recv,
     b_send,
     b_recv,
-    c_send,
-    d_send,
+    x_send,
     x_recv,
     z_send,
     z_recv,
@@ -194,25 +193,29 @@
             device_id_type=MESH,
         )
 
+    def all_sent(ref, wave, send_sems, recv_sems):
+        part = ref.at[wave, pl.ds(0, ref.shape[1] - 1)]
+        return remote(part, part, send_sems.at[wave], recv_sems.at[wave], (me + 1 - 2 * core, pos))
+
     def to_group(wave, d):
         to = lax.rem(me + d, groups)
         source = s1_ref.at[wave, to // 2, to % 2]
-        sems = a_send.at[wave, d], a_recv.at[wave, d]
+        sems = a_send.at[wave], a_recv.at[wave]
         return remote(source, r1_ref.at[wave, me], *sems, (to, pos))
 
     def to_owner(wave, d):
         to = lax.rem(pos + d, owners)
-        sems = b_send.at[wave, d], b_recv.at[wave, d]
+        sems = b_send.at[wave], b_recv.at[wave]
         return remote(s2_ref.at[wave, to], r2_ref.at[wave, pos], *sems, (me, to))
 
     def on_to_owner(wave, n):
         to = lax.rem(pos // 2 + n, owners // 2)
-        sems = c_send.at[wave, n], x_recv.at[wave, pos]
+        sems = x_send.at[wave], x_recv.at[wave]
         return remote(r1_ref.at[wave, :, to], x_ref.at[wave, pos], *sems, (me, 2 * to + core))
 
     def on_to_group(wave, n):
         to = lax.rem(z + n, chips)
-        sems = d_send.at[wave, n], x_recv.at[wave, me]
+        sems = x_send.at[wave], x_recv.at[wave]
         device = (2 * to + 1 - pos % 2, pos)
         return remote(r2_ref.at[wave, :, to], x_ref.at[wave, me], *sems, device)
 
@@ -241,17 +244,13 @@
 
     for wave in range(WAVES):
 
-        @pl.loop(1, owners)
-        def _(d, wave=wave):
-            to_owner(wave, d).wait()
+        all_sent(r2_ref, wave, b_send, b_recv).wait_recv()
 
         @pl.loop(odd, chips)
         def _(n, wave=wave):
             on_to_group(wave, n).start()
 
-        @pl.loop(1, groups)
-        def _(d, wave=wave):
-            to_group(wave, d).wait()
+        all_sent(r1_ref, wave, a_send, a_recv).wait_recv()
 
         @pl.loop(1 - odd, owners // 2)
         def _(n, wave=wave):
@@ -267,15 +266,8 @@
         for wave in range(WAVES):
             x_ref[wave, me] = r2_ref[wave, :, z]
 
-    mine = jnp.where(odd == 0, pos, me)
-
     def wave_gram(wave):
-        @pl.loop(1, owners)
-        def _(d):
-            source = lax.rem(mine + d, owners)
-            part = x_ref.at[wave, source]
-            pltpu.make_async_copy(part, part, x_recv.at[wave, source]).wait()
-
+        all_sent(x_ref, wave, x_send, x_recv).wait_recv()
         units = groups * owners
         x = x_ref[wave].astype(jnp.float32).reshape(units // 2, 2, UNIT, LANES)
         x = jnp.concatenate([x[:, 0], x[:, 1]], 1).reshape(units * UNIT, LANES)
@@ -346,15 +338,9 @@
         copy.wait_send()
 
     for wave in range(WAVES):
-
-        @pl.loop(odd, chips)
-        def _(n, wave=wave):
-            on_to_group(wave, n).wait_send()
-
-        @pl.loop(1 - odd, owners // 2)
-        def _(n, wave=wave):
-            on_to_owner(wave, n).wait_send()
-
+        all_sent(r1_ref, wave, a_send, a_recv).wait_send()
+        all_sent(r2_ref, wave, b_send, b_recv).wait_send()
+        all_sent(x_ref, wave, x_send, x_recv).wait_send()
     for wave in range(WAVES):
         for origin in range(chips):
             pair(wave, origin).wait()
@@ -414,13 +400,12 @@
             pltpu.VMEM((WAVES, groups, owners // 2, UNIT, LANES), jnp.bfloat16),
             pltpu.VMEM((WAVES, owners, groups // 2, UNIT, LANES), jnp.bfloat16),
             pltpu.VMEM((WAVES, owners, groups, UNIT, LANES), jnp.bfloat16),
-            dma((WAVES, groups)),
-            dma((WAVES, groups)),
-            dma((WAVES, owners)),
-            dma((WAVES, owners)),
-            dma((WAVES, owners // 2)),
-            dma((WAVES, groups // 2)),
-            dma((WAVES, owners)),
+            dma((WAVES,)),
+            dma((WAVES,)),
+            dma((WAVES,)),
+            dma((WAVES,)),
+            dma((WAVES,)),
+            dma((WAVES,)),
             dma((WAVES, groups // 2)),
             dma((WAVES, groups // 2)),
             dma((WAVES, groups // 2)),

time: 47.7 us -> 46 us (0.964)
  Pallas kernels: 37.4 us -> 35.7 us
    pallas_call x1, Pallas kernels: 37.4 us -> 35.7 us  [per_device(): pl.pallas_call(functools.partial(kernel, kept), out_shape=(jax.ShapeDtype...]
where the time goes in v4:
time: 46 us; the launch traced here: 45.8 us
  Pallas kernels  35.7 us (78%)
  matrix products  4.45 us (10%)
  other arithmetic  2.89 us (6%)
  between operations  1.64 us (4%)
  local copies, waits for them, and re-layouts  1.09 us (2%)
    pallas_call x1, Pallas kernels, per_device(): pl.pallas_call(functools.partial(kernel, kept), out_shape=(jax.ShapeDtype...  35.7 us
    conv_general_dilated x3, matrix products, section_out(): lax.conv_general_dilated(images, weight, (1, 1), 'SAME', dimension_number...  3.85 us
    convert_element_type x1, other arithmetic, per_device(): packets = jnp.concatenate([out.reshape(block - 1, FLAT * LANES), last.res...  1.53 us

profile of v4, /device:TPU:1, one launch (start us, length us, event | category | flops | bytes accessed | tf_op | source)
XLA Modules:
  0.0 45.8 jit_solution(15990254412005031891)
XLA Ops:
  0.6 0.0 copy-start
  0.6 0.0 copy-start.6
  0.7 0.0 copy-start.7
  0.7 0.0 copy-start.3
  0.7 0.0 copy-start.5
  1.5 0.7 %broadcast_add_fusion = (s32[128]{0:T(128)S(1)}, s32[128]{0:T(128)S(1)}, s32[128]{0:T(128)S(1)}) fusion(s32[100]{0:T(128)} %param.27), kind=kLoop, calls=%fused_computation.38 | loop fusion | flops 256 | bytes 1936 | tf_op jit(solution)/shard_map/sub | solution.py:39
  2.1 0.0 copy-done
  2.1 1.3 %fusion.12 = bf16[2,7,7,256]{3,0,2,1:T(2,128)(2,1)S(1)} fusion(bf16[2,7,7,256]{3,0,2,1:T(2,128)(2,1)} %param.17, bf16[3,3,256,256]{3,2,1,0:T(8,128)(2,1)S(1)} %copy-done, f32[256]{0:T(256)} %param.26, f32[256]{0:T(256)} %param.23, bf16[2]{0:T(256)(128)(2,1)S(1)} %compare_convert_fusion), kind=kOutput, calls=%fused_computation.18 | convolution fusion | flops 94759424 | bytes 1282052 | tf_op jit(solution)/shard_map/conv_general_dilated | solution.py:26
  3.5 0.0 copy-start.2
  3.5 0.0 copy-start.4
  3.5 0.0 copy-start.8
  3.5 0.0 copy-start.9
  3.5 0.2 convolution_convert_fusion.2
  3.7 0.0 copy-done.6
  3.7 0.0 copy-done.7
  3.7 0.0 copy-done.3
  3.7 0.0 copy-done.5
  3.8 0.7 %fusion.8 = bf16[2,14,14,128]{3,0,2,1:T(2,128)(2,1)S(1)} fusion(bf16[2,14,14,128]{3,0,2,1:T(2,128)(2,1)S(1)} %copy-done.5, bf16[3,3,128,128]{3,2,1,0:T(8,128)(2,1)S(1)} %copy-done.3, f32[128]{0:T(128)S(1)} %copy-done.6, f32[128]{0:T(128)S(1)} %copy-done.7, bf16[2]{0:T(256)(128)(2,1)S(1)} %compare_convert_fusion), kind=kOutput, calls=%fused_computation.13 | convolution fusion | flops 105108480 | bytes 496644 | tf_op jit(solution)/shard_map/conv_general_dilated | solution.py:26
  4.4 0.2 convolution_convert_fusion.1
  4.6 0.0 copy-done.2
  4.6 0.0 copy-done.4
  4.7 0.0 copy-done.8
  4.7 0.0 copy-done.9
  4.7 1.9 %fusion.13 = bf16[2,28,28,64]{3,0,2,1:T(2,128)(2,1)S(1)} fusion(bf16[2,28,28,64]{3,0,2,1:T(2,128)(2,1)S(1)} %copy-done.2, bf16[3,3,64,64]{3,2,1,0:T(8,128)(2,1)S(1)} %copy-done.4, f32[64]{0:T(128)S(1)} %copy-done.8, f32[64]{0:T(128)S(1)} %copy-done.9, bf16[2]{0:T(256)(128)(2,1)S(1)} %compare_convert_fusion), kind=kOutput, calls=%fused_computation.20 | convolution fusion | flops 110667776 | bytes 475652 | tf_op jit(solution)/shard_map/conv_general_dilated | solution.py:26
  6.5 0.0 copy-start.1
  6.5 0.3 fusion.3
  6.8 0.1 pad.17.f1_ref
  6.9 0.5 %copy-done.1 = s32[128,128]{1,0:T(8,128)S(1)} copy-done((s32[128,128]{1,0:T(8,128)S(1)}, s32[128,128]{1,0:T(8,128)}, u32[]{:S(2)}) %copy-start.1) | copy-done | bytes 65560
  7.4 35.7 %statistics.1 = (bf16[16,240,128]{2,1,0:T(8,128)(2,1)S(1)}, bf16[80,128]{1,0:T(8,128)(2,1)S(1)}) custom-call(bf16[2,29,32,128]{3,2,1,0:T(8,128)(2,1)S(1)} %pad.17.f1_ref, bf16[2,16,16,128]{3,2,1,0:T(8,128)(2,1)S(1)} %pad.18.f2_ref, bf16[2,8,16,128]{3,2,1,0:T(8,128)(2,1)S(1)} %pad.19.f3_ref, s32[128,128]{1,0:T(8,128)S(1)} %copy-done.1), custom_call_target="tpu_custom_call" | custom-call | flops 800000000 | bytes 4000000 | tf_op jit(solution)/shard_map/statistics/pallas_call | solution.py:387
  43.1 0.4 reshape.26
  43.6 0.7 %fusion.25 = f32[100,49]{0,1:T(8,128)} fusion(bf16[1,10240]{1,0:T(2,128)(2,1)S(1)} %bitcast.31, bf16[48,10240]{1,0:T(8,128)(2,1)S(1)} %reshape.26), kind=kLoop, calls=%fused_computation.34 | loop fusion | flops 44100 | bytes 1023120 | tf_op jit(solution)/shard_map/transpose | solution.py:429
  44.3 1.5 %fusion.7 = f32[49,10000]{1,0:T(8,128)} fusion(bf16[1,10240]{1,0:T(2,128)(2,1)S(1)} %bitcast.32, bf16[48,10240]{1,0:T(8,128)(2,1)S(1)} %reshape.26), kind=kLoop, calls=%fused_computation.12 | loop fusion | flops 1960000 | bytes 2963520 | tf_op jit(solution)/shard_map/convert_element_type | solution.py:424
  (5 shorter events, 0.1 us)
Async XLA Ops:
  0.6 1.5 %copy-start = (bf16[3,3,256,256]{3,2,1,0:T(8,128)(2,1)S(1)}, bf16[3,3,256,256]{3,2,1,0:T(8,128)(2,1)}, u32[]{:S(2)}) copy-start(bf16[3,3,256,256]{3,2,1,0:T(8,128)(2,1)} %param.20) | copy-start | bytes 3538948
  0.6 3.1 %copy-start.6 = (f32[128]{0:T(128)S(1)}, f32[128]{0:T(128)}, u32[]{:S(2)}) copy-start(f32[128]{0:T(128)} %param.25) | copy-start | bytes 1540
  0.7 3.1 %copy-start.7 = (f32[128]{0:T(128)S(1)}, f32[128]{0:T(128)}, u32[]{:S(2)}) copy-start(f32[128]{0:T(128)} %param.22) | copy-start | bytes 1540
  0.7 3.1 %copy-start.3 = (bf16[3,3,128,128]{3,2,1,0:T(8,128)(2,1)S(1)}, bf16[3,3,128,128]{3,2,1,0:T(8,128)(2,1)}, u32[]{:S(2)}) copy-start(bf16[3,3,128,128]{3,2,1,0:T(8,128)(2,1)} %param.19) | copy-start | bytes 884740
  0.7 3.1 %copy-start.5 = (bf16[2,14,14,128]{3,0,2,1:T(2,128)(2,1)S(1)}, bf16[2,14,14,128]{3,0,2,1:T(2,128)(2,1)}, u32[]{:S(2)}) copy-start(bf16[2,14,14,128]{3,0,2,1:T(2,128)(2,1)} %param.16) | copy-start | bytes 301060
  3.5 1.2 %copy-start.2 = (bf16[2,28,28,64]{3,0,2,1:T(2,128)(2,1)S(1)}, bf16[2,28,28,64]{3,0,2,1:T(2,128)(2,1)}, u32[]{:S(2)}) copy-start(bf16[2,28,28,64]{3,0,2,1:T(2,128)(2,1)} %param.15) | copy-start | bytes 602116
  3.5 1.2 %copy-start.4 = (bf16[3,3,64,64]{3,2,1,0:T(8,128)(2,1)S(1)}, bf16[3,3,64,64]{3,2,1,0:T(8,128)(2,1)}, u32[]{:S(2)}) copy-start(bf16[3,3,64,64]{3,2,1,0:T(8,128)(2,1)} %param.18) | copy-start | bytes 221188
  3.5 1.2 %copy-start.8 = (f32[64]{0:T(128)S(1)}, f32[64]{0:T(128)}, u32[]{:S(2)}) copy-start(f32[64]{0:T(128)} %param.24) | copy-start | bytes 772
  3.5 1.2 %copy-start.9 = (f32[64]{0:T(128)S(1)}, f32[64]{0:T(128)}, u32[]{:S(2)}) copy-start(f32[64]{0:T(128)} %param.21) | copy-start | bytes 772
  6.5 0.8 %copy-start.1 = (s32[128,128]{1,0:T(8,128)S(1)}, s32[128,128]{1,0:T(8,128)}, u32[]{:S(2)}) copy-start(s32[128,128]{1,0:T(8,128)} %constant.22.clone.index_hbm) | copy-start | bytes 196612

commit v5 on v4

--- a/solution.py
+++ b/solution.py
@@ -283,38 +283,31 @@
     def slot_at(distance):
         return lax.rem(z + chips - distance, chips) * 2 + core
 
-    def share(rows, origin, target, sems, send, came):
+    def share(rows, origin, target, wave, came):
         part = out_ref.at[slot_at(origin), pl.ds(*rows)]
         device = (lax.rem(z + target, chips) * 2 + core, pos)
-        return remote(part, part, z_send.at[sems, send], z_recv.at[sems, came], device)
+        return remote(part, part, z_send, z_recv.at[wave, came], device)
 
     def pair(wave, origin):
         part = out_ref.at[slot_at(origin), pl.ds(*WHOLE[wave])]
-        sems = pair_send.at[wave, origin], pair_recv.at[wave, origin]
-        return remote(part, part, *sems, (z * 2 + 1 - core, pos))
-
-    sent = []
+        return remote(part, part, pair_send, pair_recv, (z * 2 + 1 - core, pos))
 
     def begin(wave):
         for target in (2, 6, 1, 7):
-            sent.append(share(WHOLE[wave], 0, target, wave, target, target))
-            sent[-1].start()
+            share(WHOLE[wave], 0, target, wave, target).start()
 
     def arrive(wave, origin):
         if origin == 4:
-            share(LOWER[wave], 4, 1, wave, 0, 4).wait_recv()
-            share(UPPER[wave], 4, 1, wave, 0, 0).wait_recv()
+            share(LOWER[wave], 4, 1, wave, 4).wait_recv()
+            share(UPPER[wave], 4, 1, wave, 0).wait_recv()
         else:
-            share(WHOLE[wave], origin, 1, wave, 0, origin).wait_recv()
+            share(WHOLE[wave], origin, 1, wave, origin).wait_recv()
         if origin == 2:
-            sent.append(share(LOWER[wave], 2, 2, wave, 4, 4))
-            sent.append(share(WHOLE[wave], 2, 1, wave, 3, 3))
+            share(LOWER[wave], 2, 2, wave, 4).start()
+            share(WHOLE[wave], 2, 1, wave, 3).start()
         elif origin == 6:
-            sent.append(share(UPPER[wave], 6, 6, wave, 0, 0))
-            sent.append(share(WHOLE[wave], 6, 7, wave, 5, 5))
-        if origin in (2, 6):
-            sent[-2].start()
-            sent[-1].start()
+            share(UPPER[wave], 6, 6, wave, 0).start()
+            share(WHOLE[wave], 6, 7, wave, 5).start()
         pair(wave, origin).start()
 
     for q in range(SLOTS - 1):
@@ -334,16 +327,16 @@
     for wave in range(WAVES):
         for origin in (3, 5, 4):
             arrive(wave, origin)
-    for copy in sent:
-        copy.wait_send()
+    partner = (z * 2 + 1 - core, pos)
+    part = out_ref.at[pl.ds(0, chips - 1)]
+    remote(part, part, z_send, pair_recv, partner).wait_send()
 
     for wave in range(WAVES):
         all_sent(r1_ref, wave, a_send, a_recv).wait_send()
         all_sent(r2_ref, wave, b_send, b_recv).wait_send()
         all_sent(x_ref, wave, x_send, x_recv).wait_send()
-    for wave in range(WAVES):
-        for origin in range(chips):
-            pair(wave, origin).wait()
+    part = out_ref.at[pl.ds(0, chips)]
+    remote(part, part, pair_send, pair_recv, partner).wait()
 
 
 def per_device(
@@ -406,10 +399,10 @@
             dma((WAVES,)),
             dma((WAVES,)),
             dma((WAVES,)),
+            dma(()),
             dma((WAVES, groups // 2)),
-            dma((WAVES, groups // 2)),
-            dma((WAVES, groups // 2)),
-            dma((WAVES, groups // 2)),
+            dma(()),
+            dma(()),
         ],
         compiler_params=pltpu.CompilerParams(
             collective_id=0, has_side_effects=True, vmem_limit_bytes=40 * 2**20

time: 46 us -> 45.6 us (level)
  no operation moved by 1% of the time
where the time goes in v5:
time: 45.6 us; the launch traced here: 45.4 us
  Pallas kernels  35.3 us (77%)
  matrix products  4.45 us (10%)
  other arithmetic  2.89 us (6%)
  between operations  1.64 us (4%)
  local copies, waits for them, and re-layouts  1.09 us (2%)
    pallas_call x1, Pallas kernels, per_device(): pl.pallas_call(functools.partial(kernel, kept), out_shape=(jax.ShapeDtype...  35.3 us
    conv_general_dilated x3, matrix products, section_out(): lax.conv_general_dilated(images, weight, (1, 1), 'SAME', dimension_number...  3.85 us
    convert_element_type x1, other arithmetic, per_device(): packets = jnp.concatenate([out.reshape(block - 1, FLAT * LANES), last.res...  1.53 us

profile of v5, /device:TPU:1, one launch (start us, length us, event | category | flops | bytes accessed | tf_op | source)
XLA Modules:
  0.0 45.4 jit_solution(158930618126149414)
XLA Ops:
  0.6 0.0 copy-start
  0.6 0.0 copy-start.6
  0.7 0.0 copy-start.7
  0.7 0.0 copy-start.3
  0.7 0.0 copy-start.5
  1.5 0.7 %broadcast_add_fusion = (s32[128]{0:T(128)S(1)}, s32[128]{0:T(128)S(1)}, s32[128]{0:T(128)S(1)}) fusion(s32[100]{0:T(128)} %param.27), kind=kLoop, calls=%fused_computation.38 | loop fusion | flops 256 | bytes 1936 | tf_op jit(solution)/shard_map/sub | solution.py:39
  2.1 0.0 copy-done
  2.1 1.3 %fusion.12 = bf16[2,7,7,256]{3,0,2,1:T(2,128)(2,1)S(1)} fusion(bf16[2,7,7,256]{3,0,2,1:T(2,128)(2,1)} %param.17, bf16[3,3,256,256]{3,2,1,0:T(8,128)(2,1)S(1)} %copy-done, f32[256]{0:T(256)} %param.26, f32[256]{0:T(256)} %param.23, bf16[2]{0:T(256)(128)(2,1)S(1)} %compare_convert_fusion), kind=kOutput, calls=%fused_computation.18 | convolution fusion | flops 94759424 | bytes 1282052 | tf_op jit(solution)/shard_map/conv_general_dilated | solution.py:26
  3.5 0.0 copy-start.2
  3.5 0.0 copy-start.4
  3.5 0.0 copy-start.8
  3.5 0.0 copy-start.9
  3.5 0.2 convolution_convert_fusion.2
  3.7 0.0 copy-done.6
  3.7 0.0 copy-done.7
  3.7 0.0 copy-done.3
  3.7 0.0 copy-done.5
  3.8 0.7 %fusion.8 = bf16[2,14,14,128]{3,0,2,1:T(2,128)(2,1)S(1)} fusion(bf16[2,14,14,128]{3,0,2,1:T(2,128)(2,1)S(1)} %copy-done.5, bf16[3,3,128,128]{3,2,1,0:T(8,128)(2,1)S(1)} %copy-done.3, f32[128]{0:T(128)S(1)} %copy-done.6, f32[128]{0:T(128)S(1)} %copy-done.7, bf16[2]{0:T(256)(128)(2,1)S(1)} %compare_convert_fusion), kind=kOutput, calls=%fused_computation.13 | convolution fusion | flops 105108480 | bytes 496644 | tf_op jit(solution)/shard_map/conv_general_dilated | solution.py:26
  4.4 0.2 convolution_convert_fusion.1
  4.6 0.0 copy-done.2
  4.6 0.0 copy-done.4
  4.7 0.0 copy-done.8
  4.7 0.0 copy-done.9
  4.7 1.9 %fusion.13 = bf16[2,28,28,64]{3,0,2,1:T(2,128)(2,1)S(1)} fusion(bf16[2,28,28,64]{3,0,2,1:T(2,128)(2,1)S(1)} %copy-done.2, bf16[3,3,64,64]{3,2,1,0:T(8,128)(2,1)S(1)} %copy-done.4, f32[64]{0:T(128)S(1)} %copy-done.8, f32[64]{0:T(128)S(1)} %copy-done.9, bf16[2]{0:T(256)(128)(2,1)S(1)} %compare_convert_fusion), kind=kOutput, calls=%fused_computation.20 | convolution fusion | flops 110667776 | bytes 475652 | tf_op jit(solution)/shard_map/conv_general_dilated | solution.py:26
  6.5 0.0 copy-start.1
  6.5 0.3 fusion.3
  6.8 0.1 pad.17.f1_ref
  6.9 0.5 %copy-done.1 = s32[128,128]{1,0:T(8,128)S(1)} copy-done((s32[128,128]{1,0:T(8,128)S(1)}, s32[128,128]{1,0:T(8,128)}, u32[]{:S(2)}) %copy-start.1) | copy-done | bytes 65560
  7.4 35.3 %statistics.1 = (bf16[16,240,128]{2,1,0:T(8,128)(2,1)S(1)}, bf16[80,128]{1,0:T(8,128)(2,1)S(1)}) custom-call(bf16[2,29,32,128]{3,2,1,0:T(8,128)(2,1)S(1)} %pad.17.f1_ref, bf16[2,16,16,128]{3,2,1,0:T(8,128)(2,1)S(1)} %pad.18.f2_ref, bf16[2,8,16,128]{3,2,1,0:T(8,128)(2,1)S(1)} %pad.19.f3_ref, s32[128,128]{1,0:T(8,128)S(1)} %copy-done.1), custom_call_target="tpu_custom_call" | custom-call | flops 800000000 | bytes 4000000 | tf_op jit(solution)/shard_map/statistics/pallas_call | solution.py:380
  42.7 0.4 reshape.26
  43.2 0.7 %fusion.25 = f32[100,49]{0,1:T(8,128)} fusion(bf16[1,10240]{1,0:T(2,128)(2,1)S(1)} %bitcast.31, bf16[48,10240]{1,0:T(8,128)(2,1)S(1)} %reshape.26), kind=kLoop, calls=%fused_computation.34 | loop fusion | flops 44100 | bytes 1023120 | tf_op jit(solution)/shard_map/transpose | solution.py:422
  43.9 1.5 %fusion.7 = f32[49,10000]{1,0:T(8,128)} fusion(bf16[1,10240]{1,0:T(2,128)(2,1)S(1)} %bitcast.32, bf16[48,10240]{1,0:T(8,128)(2,1)S(1)} %reshape.26), kind=kLoop, calls=%fused_computation.12 | loop fusion | flops 1960000 | bytes 2963520 | tf_op jit(solution)/shard_map/convert_element_type | solution.py:417
  (5 shorter events, 0.1 us)
Async XLA Ops:
  0.6 1.5 %copy-start = (bf16[3,3,256,256]{3,2,1,0:T(8,128)(2,1)S(1)}, bf16[3,3,256,256]{3,2,1,0:T(8,128)(2,1)}, u32[]{:S(2)}) copy-start(bf16[3,3,256,256]{3,2,1,0:T(8,128)(2,1)} %param.20) | copy-start | bytes 3538948
  0.6 3.1 %copy-start.6 = (f32[128]{0:T(128)S(1)}, f32[128]{0:T(128)}, u32[]{:S(2)}) copy-start(f32[128]{0:T(128)} %param.25) | copy-start | bytes 1540
  0.7 3.1 %copy-start.7 = (f32[128]{0:T(128)S(1)}, f32[128]{0:T(128)}, u32[]{:S(2)}) copy-start(f32[128]{0:T(128)} %param.22) | copy-start | bytes 1540
  0.7 3.1 %copy-start.3 = (bf16[3,3,128,128]{3,2,1,0:T(8,128)(2,1)S(1)}, bf16[3,3,128,128]{3,2,1,0:T(8,128)(2,1)}, u32[]{:S(2)}) copy-start(bf16[3,3,128,128]{3,2,1,0:T(8,128)(2,1)} %param.19) | copy-start | bytes 884740
  0.7 3.1 %copy-start.5 = (bf16[2,14,14,128]{3,0,2,1:T(2,128)(2,1)S(1)}, bf16[2,14,14,128]{3,0,2,1:T(2,128)(2,1)}, u32[]{:S(2)}) copy-start(bf16[2,14,14,128]{3,0,2,1:T(2,128)(2,1)} %param.16) | copy-start | bytes 301060
  3.5 1.2 %copy-start.2 = (bf16[2,28,28,64]{3,0,2,1:T(2,128)(2,1)S(1)}, bf16[2,28,28,64]{3,0,2,1:T(2,128)(2,1)}, u32[]{:S(2)}) copy-start(bf16[2,28,28,64]{3,0,2,1:T(2,128)(2,1)} %param.15) | copy-start | bytes 602116
  3.5 1.2 %copy-start.4 = (bf16[3,3,64,64]{3,2,1,0:T(8,128)(2,1)S(1)}, bf16[3,3,64,64]{3,2,1,0:T(8,128)(2,1)}, u32[]{:S(2)}) copy-start(bf16[3,3,64,64]{3,2,1,0:T(8,128)(2,1)} %param.18) | copy-start | bytes 221188
  3.5 1.2 %copy-start.8 = (f32[64]{0:T(128)S(1)}, f32[64]{0:T(128)}, u32[]{:S(2)}) copy-start(f32[64]{0:T(128)} %param.24) | copy-start | bytes 772
  3.5 1.2 %copy-start.9 = (f32[64]{0:T(128)S(1)}, f32[64]{0:T(128)}, u32[]{:S(2)}) copy-start(f32[64]{0:T(128)} %param.21) | copy-start | bytes 772
  6.5 0.8 %copy-start.1 = (s32[128,128]{1,0:T(8,128)S(1)}, s32[128,128]{1,0:T(8,128)}, u32[]{:S(2)}) copy-start(s32[128,128]{1,0:T(8,128)} %constant.22.clone.index_hbm) | copy-start | bytes 196612

commit v6 on v5

--- a/solution.py
+++ b/solution.py
@@ -320,10 +320,10 @@
             pair(0, 0).start()
     begin(1)
     pair(1, 0).start()
-    last_ref[...] = packets(kept, gram, picks, masks, PER_WAVE - 1)
     for wave in range(WAVES):
         for origin in (2, 6, 1, 7):
             arrive(wave, origin)
+    last_ref[...] = packets(kept, gram, picks, masks, PER_WAVE - 1)
     for wave in range(WAVES):
         for origin in (3, 5, 4):
             arrive(wave, origin)

time: 45.6 us -> 45.6 us (level)
  no operation moved by 1% of the time
where the time goes in v6:
time: 45.6 us; the launch traced here: 45.4 us
  Pallas kernels  35.3 us (77%)
  matrix products  4.45 us (10%)
  other arithmetic  2.89 us (6%)
  between operations  1.64 us (4%)
  local copies, waits for them, and re-layouts  1.09 us (2%)
    pallas_call x1, Pallas kernels, per_device(): pl.pallas_call(functools.partial(kernel, kept), out_shape=(jax.ShapeDtype...  35.3 us
    conv_general_dilated x3, matrix products, section_out(): lax.conv_general_dilated(images, weight, (1, 1), 'SAME', dimension_number...  3.85 us
    convert_element_type x1, other arithmetic, per_device(): packets = jnp.concatenate([out.reshape(block - 1, FLAT * LANES), last.res...  1.53 us

profile of v6, /device:TPU:1, one launch (start us, length us, event | category | flops | bytes accessed | tf_op | source)
XLA Modules:
  0.0 45.4 jit_solution(580796139975950217)
XLA Ops:
  0.6 0.0 copy-start
  0.6 0.0 copy-start.6
  0.7 0.0 copy-start.7
  0.7 0.0 copy-start.3
  0.7 0.0 copy-start.5
  1.5 0.7 %broadcast_add_fusion = (s32[128]{0:T(128)S(1)}, s32[128]{0:T(128)S(1)}, s32[128]{0:T(128)S(1)}) fusion(s32[100]{0:T(128)} %param.27), kind=kLoop, calls=%fused_computation.38 | loop fusion | flops 256 | bytes 1936 | tf_op jit(solution)/shard_map/sub | solution.py:39
  2.1 0.0 copy-done
  2.1 1.3 %fusion.12 = bf16[2,7,7,256]{3,0,2,1:T(2,128)(2,1)S(1)} fusion(bf16[2,7,7,256]{3,0,2,1:T(2,128)(2,1)} %param.17, bf16[3,3,256,256]{3,2,1,0:T(8,128)(2,1)S(1)} %copy-done, f32[256]{0:T(256)} %param.26, f32[256]{0:T(256)} %param.23, bf16[2]{0:T(256)(128)(2,1)S(1)} %compare_convert_fusion), kind=kOutput, calls=%fused_computation.18 | convolution fusion | flops 94759424 | bytes 1282052 | tf_op jit(solution)/shard_map/conv_general_dilated | solution.py:26
  3.5 0.0 copy-start.2
  3.5 0.0 copy-start.4
  3.5 0.0 copy-start.8
  3.5 0.0 copy-start.9
  3.5 0.2 convolution_convert_fusion.2
  3.7 0.0 copy-done.6
  3.7 0.0 copy-done.7
  3.7 0.0 copy-done.3
  3.7 0.0 copy-done.5
  3.8 0.7 %fusion.8 = bf16[2,14,14,128]{3,0,2,1:T(2,128)(2,1)S(1)} fusion(bf16[2,14,14,128]{3,0,2,1:T(2,128)(2,1)S(1)} %copy-done.5, bf16[3,3,128,128]{3,2,1,0:T(8,128)(2,1)S(1)} %copy-done.3, f32[128]{0:T(128)S(1)} %copy-done.6, f32[128]{0:T(128)S(1)} %copy-done.7, bf16[2]{0:T(256)(128)(2,1)S(1)} %compare_convert_fusion), kind=kOutput, calls=%fused_computation.13 | convolution fusion | flops 105108480 | bytes 496644 | tf_op jit(solution)/shard_map/conv_general_dilated | solution.py:26
  4.4 0.2 convolution_convert_fusion.1
  4.6 0.0 copy-done.2
  4.6 0.0 copy-done.4
  4.7 0.0 copy-done.8
  4.7 0.0 copy-done.9
  4.7 1.9 %fusion.13 = bf16[2,28,28,64]{3,0,2,1:T(2,128)(2,1)S(1)} fusion(bf16[2,28,28,64]{3,0,2,1:T(2,128)(2,1)S(1)} %copy-done.2, bf16[3,3,64,64]{3,2,1,0:T(8,128)(2,1)S(1)} %copy-done.4, f32[64]{0:T(128)S(1)} %copy-done.8, f32[64]{0:T(128)S(1)} %copy-done.9, bf16[2]{0:T(256)(128)(2,1)S(1)} %compare_convert_fusion), kind=kOutput, calls=%fused_computation.20 | convolution fusion | flops 110667776 | bytes 475652 | tf_op jit(solution)/shard_map/conv_general_dilated | solution.py:26
  6.5 0.0 copy-start.1
  6.5 0.3 fusion.3
  6.8 0.1 pad.17.f1_ref
  6.9 0.5 %copy-done.1 = s32[128,128]{1,0:T(8,128)S(1)} copy-done((s32[128,128]{1,0:T(8,128)S(1)}, s32[128,128]{1,0:T(8,128)}, u32[]{:S(2)}) %copy-start.1) | copy-done | bytes 65560
  7.4 35.3 %statistics.1 = (bf16[16,240,128]{2,1,0:T(8,128)(2,1)S(1)}, bf16[80,128]{1,0:T(8,128)(2,1)S(1)}) custom-call(bf16[2,29,32,128]{3,2,1,0:T(8,128)(2,1)S(1)} %pad.17.f1_ref, bf16[2,16,16,128]{3,2,1,0:T(8,128)(2,1)S(1)} %pad.18.f2_ref, bf16[2,8,16,128]{3,2,1,0:T(8,128)(2,1)S(1)} %pad.19.f3_ref, s32[128,128]{1,0:T(8,128)S(1)} %copy-done.1), custom_call_target="tpu_custom_call" | custom-call | flops 800000000 | bytes 4000000 | tf_op jit(solution)/shard_map/statistics/pallas_call | solution.py:380
  42.7 0.4 reshape.26
  43.2 0.7 %fusion.25 = f32[100,49]{0,1:T(8,128)} fusion(bf16[1,10240]{1,0:T(2,128)(2,1)S(1)} %bitcast.31, bf16[48,10240]{1,0:T(8,128)(2,1)S(1)} %reshape.26), kind=kLoop, calls=%fused_computation.34 | loop fusion | flops 44100 | bytes 1023120 | tf_op jit(solution)/shard_map/transpose | solution.py:422
  43.9 1.5 %fusion.7 = f32[49,10000]{1,0:T(8,128)} fusion(bf16[1,10240]{1,0:T(2,128)(2,1)S(1)} %bitcast.32, bf16[48,10240]{1,0:T(8,128)(2,1)S(1)} %reshape.26), kind=kLoop, calls=%fused_computation.12 | loop fusion | flops 1960000 | bytes 2963520 | tf_op jit(solution)/shard_map/convert_element_type | solution.py:417
  (5 shorter events, 0.1 us)
Async XLA Ops:
  0.6 1.5 %copy-start = (bf16[3,3,256,256]{3,2,1,0:T(8,128)(2,1)S(1)}, bf16[3,3,256,256]{3,2,1,0:T(8,128)(2,1)}, u32[]{:S(2)}) copy-start(bf16[3,3,256,256]{3,2,1,0:T(8,128)(2,1)} %param.20) | copy-start | bytes 3538948
  0.6 3.1 %copy-start.6 = (f32[128]{0:T(128)S(1)}, f32[128]{0:T(128)}, u32[]{:S(2)}) copy-start(f32[128]{0:T(128)} %param.25) | copy-start | bytes 1540
  0.7 3.1 %copy-start.7 = (f32[128]{0:T(128)S(1)}, f32[128]{0:T(128)}, u32[]{:S(2)}) copy-start(f32[128]{0:T(128)} %param.22) | copy-start | bytes 1540
  0.7 3.1 %copy-start.3 = (bf16[3,3,128,128]{3,2,1,0:T(8,128)(2,1)S(1)}, bf16[3,3,128,128]{3,2,1,0:T(8,128)(2,1)}, u32[]{:S(2)}) copy-start(bf16[3,3,128,128]{3,2,1,0:T(8,128)(2,1)} %param.19) | copy-start | bytes 884740
  0.7 3.1 %copy-start.5 = (bf16[2,14,14,128]{3,0,2,1:T(2,128)(2,1)S(1)}, bf16[2,14,14,128]{3,0,2,1:T(2,128)(2,1)}, u32[]{:S(2)}) copy-start(bf16[2,14,14,128]{3,0,2,1:T(2,128)(2,1)} %param.16) | copy-start | bytes 301060
  3.5 1.2 %copy-start.2 = (bf16[2,28,28,64]{3,0,2,1:T(2,128)(2,1)S(1)}, bf16[2,28,28,64]{3,0,2,1:T(2,128)(2,1)}, u32[]{:S(2)}) copy-start(bf16[2,28,28,64]{3,0,2,1:T(2,128)(2,1)} %param.15) | copy-start | bytes 602116
  3.5 1.2 %copy-start.4 = (bf16[3,3,64,64]{3,2,1,0:T(8,128)(2,1)S(1)}, bf16[3,3,64,64]{3,2,1,0:T(8,128)(2,1)}, u32[]{:S(2)}) copy-start(bf16[3,3,64,64]{3,2,1,0:T(8,128)(2,1)} %param.18) | copy-start | bytes 221188
  3.5 1.2 %copy-start.8 = (f32[64]{0:T(128)S(1)}, f32[64]{0:T(128)}, u32[]{:S(2)}) copy-start(f32[64]{0:T(128)} %param.24) | copy-start | bytes 772
  3.5 1.2 %copy-start.9 = (f32[64]{0:T(128)S(1)}, f32[64]{0:T(128)}, u32[]{:S(2)}) copy-start(f32[64]{0:T(128)} %param.21) | copy-start | bytes 772
  6.5 0.8 %copy-start.1 = (s32[128,128]{1,0:T(8,128)S(1)}, s32[128,128]{1,0:T(8,128)}, u32[]{:S(2)}) copy-start(s32[128,128]{1,0:T(8,128)} %constant.22.clone.index_hbm) | copy-start | bytes 196612
